TPU v7x, 32 devices: a whole 2x2x4 slice. The times are simulated.
32 devices in a mesh: groups: 2 (over x), row: 16 (over z, y, core).
Axes of the slice: x: 2, y: 2, z: 4, core: 2. Of those that a mesh axis runs over, the one named last changes fastest.
Arguments:
- forces: bfloat16 [2048, 768], P(('groups', 'row')), parts along dimension 0, may hold values from -6 to 6
- tiles: bfloat16 [32768, 96, 96], P(('groups', 'row')), parts along dimension 0, may hold values from -0.109375 to 0.109375
- tile_local: int32 [32768], P(('groups', 'row')), parts along dimension 0, may hold values from 0 to 63
- tile_slot: int32 [32768], P(('groups', 'row')), parts along dimension 0, may hold values from 0 to 255
- tile_flag: int32 [32768], P(('groups', 'row')), parts along dimension 0, may hold values 0 or 1
- want_list: int32 [32, 16, 16], P(('groups', 'row')), parts along dimension 0, may hold values from 0 to 63
Outputs:
- krylov_one: bfloat16 [2048, 768], P(('groups', 'row')), parts along dimension 0
- krylov_two: bfloat16 [2048, 768], P(('groups', 'row')), parts along dimension 0
There are 2 independent parts, one for each index of `groups`. A program takes and returns all parts, laid end to end along the dimension named above; each array names one. Nothing has to cross between parts.
All inputs are finite; a program needn't handle non-finite values. No bound on the sum of `tile_flag` on one device may be relied on, other than what follows from the above.
Results may differ from a plain program's by a relative error of at most 0.0041.
Values may be sent and summed in bfloat16 or wider, within the bound.
A program may use at most 128 MiB of HBM per device.

v0:
```python
import jax
import jax.numpy as jnp
from jax import lax
from jax.sharding import PartitionSpec as P

NRHS = 8


def one_hot_table(index, count, kind):
    return (index[:, None] == jnp.arange(count, dtype=jnp.int32)[None, :]).astype(kind)


def pick_rows(table, values):
    return jnp.dot(table, values, preferred_element_type=jnp.float32).astype(jnp.bfloat16)


def sum_rows(table, partial_rows):
    return lax.dot_general(
        table,
        partial_rows,
        (((0,), (0,)), ((), ())),
        precision=lax.Precision.HIGHEST,
        preferred_element_type=jnp.float32,
    )


def per_device(forces, tiles, tile_local, tile_slot, tile_flag, want_list):
    peer_count = lax.axis_size("row")
    fibres = forces.shape[0]
    row_width = forces.shape[1]
    unknowns = tiles.shape[1]
    capacity = want_list.shape[2]
    blocks = tiles.shape[0]
    slot_total = peer_count * capacity
    wanted = want_list[0]
    mirror_gate = tile_flag.astype(jnp.float32)[:, None, None]
    local_pick = one_hot_table(tile_local, fibres, jnp.bfloat16)
    local_sum = one_hot_table(tile_local, fibres, jnp.float32)
    slot_pick = one_hot_table(tile_slot, slot_total, jnp.bfloat16)
    slot_sum = one_hot_table(tile_slot, slot_total, jnp.float32)
    global_rows = (jnp.arange(peer_count, dtype=jnp.int32)[:, None] * fibres + wanted).reshape(-1)
    global_pick = one_hot_table(global_rows, fibres * peer_count, jnp.bfloat16)
    global_sum = one_hot_table(global_rows, fibres * peer_count, jnp.float32)

    def operate(current):
        own_forces = pick_rows(local_pick, current).reshape(blocks, NRHS, unknowns)
        mirror = (
            jnp.einsum("kij,kri->krj", tiles, own_forces, preferred_element_type=jnp.float32)
            * mirror_gate
        )
        slot_part = sum_rows(slot_sum, mirror.reshape(blocks, row_width))
        all_rows = lax.all_gather(current, "row", axis=0, tiled=True)
        slot_forces = pick_rows(global_pick, all_rows)
        far_forces = pick_rows(slot_pick, slot_forces).reshape(blocks, NRHS, unknowns)
        direct = jnp.einsum("kij,krj->kri", tiles, far_forces, preferred_element_type=jnp.float32)
        own_part = sum_rows(local_sum, direct.reshape(blocks, row_width))
        dense_part = sum_rows(global_sum, slot_part)
        returned = lax.psum_scatter(dense_part, "row", scatter_dimension=0, tiled=True)
        return (own_part + returned).astype(jnp.bfloat16)

    krylov_one = operate(forces)
    krylov_two = operate(krylov_one)
    return (krylov_one, krylov_two)


def solution(mesh):
    in_specs = (
        P(("groups", "row"), None),
        P(("groups", "row"), None, None),
        P(("groups", "row")),
        P(("groups", "row")),
        P(("groups", "row")),
        P(("groups", "row"), None, None),
    )
    out_specs = (P(("groups", "row"), None), P(("groups", "row"), None))
    return jax.shard_map(
        per_device, mesh=mesh, in_specs=in_specs, out_specs=out_specs, check_vma=False
    )
```

profile of v0, /device:TPU:9, one launch (start us, length us, event | category | flops | bytes accessed | tf_op | source)
XLA Modules:
  0.0 253.1 jit_solution(7490937594834433806)
XLA Ops:
  7.2 0.0 all-gather.3.cloned.1.call-start
  7.2 0.7 all-gather.3.cloned.1.call-update
  7.9 0.0 copy-start.4
  7.9 0.0 copy-start
  7.9 0.0 copy-start.1
  7.9 0.0 reduce-scatter.3.cloned.1.call-start
  8.0 29.6 %copy.17 = bf16[1024,96,96]{2,1,0:T(8,128)(2,1)} copy(bf16[1024,96,96]{0,2,1:T(8,128)(2,1)} %param.7) | data formatting | bytes 37748736 | tf_op args[1]
  37.6 0.0 copy-done.4
  37.6 0.0 copy-done
  37.6 0.0 copy-done.1
  37.6 1.9 convolution_convert_fusion.1
  39.5 3.3 %copy.19 = bf16[1024,8,96]{2,1,0:T(8,128)(2,1)S(1)} copy(bf16[1024,8,96]{0,2,1:T(8,128)(2,1)} %bitcast.30) | data formatting | bytes 3145728 | tf_op jit(solution)/shard_map/reshape | solution.py:46
  42.8 13.5 %broadcast_multiply_fusion.1 = f32[1024,8,96]{2,1,0:T(8,128)} fusion(f32[1024]{0:T(1024)S(1)} %convert_element_type.36, bf16[1024,8,96]{2,1,0:T(8,128)(2,1)S(1)} %copy.19, bf16[1024,96,96]{2,1,0:T(8,128)(2,1)} %copy.17), kind=kOutput, calls=%fused_computation.1 | convolution fusion | flops 151781376 | bytes 23597056 | tf_op jit(solution)/shard_map/kij,kri->krj/dot_general | solution.py:48
  56.4 0.0 copy-start.3
  56.4 0.0 copy-start.2
  56.4 3.9 %copy.21 = f32[1024,8,96]{0,2,1:T(8,128)S(1)} copy(f32[1024,8,96]{2,1,0:T(8,128)} %broadcast_multiply_fusion.1) | data formatting | bytes 6291456 | tf_op jit(solution)/shard_map/mul | solution.py:48
  60.3 0.1 add.24
  60.3 0.1 add.25
  60.4 0.0 copy-done.3
  60.4 0.1 squeeze.3
  60.5 0.0 copy-done.2
  60.5 2.0 fusion.7
  62.5 3.4 %fusion.3 = f32[1024,768]{1,0:T(8,128)} fusion(f32[256,768]{1,0:T(8,128)S(1)} %fusion.7, s32[256]{0:T(256)S(1)} %add.26), kind=kOutput, calls=%fused_computation.14 | convolution fusion | flops 2416181248 | bytes 3933184 | tf_op jit(solution)/shard_map/dot_general | solution.py:18
  65.9 0.0 reduce-scatter.3.cloned.1.call-update
  65.9 0.2 all-gather.5.cloned.1.call-start
  66.2 0.0 all-gather.3.cloned.1.call-done
  66.2 4.0 %convolution_convert_fusion.3 = bf16[1024,768]{0,1:T(8,128)(2,1)} fusion(bf16[1024,768]{1,0:T(8,128)(2,1)} %all-gather.3.cloned.1.call-done, s32[256]{0:T(256)S(1)} %add.26, s32[1024]{0:T(1024)S(1)} %copy-done.2), kind=kOutput, calls=%fused_computation.5 | convolution fusion | flops 806813696 | bytes 3150848 | tf_op jit(solution)/shard_map/dot_general | solution.py:14
  70.2 3.3 %copy.16 = bf16[1024,8,96]{2,1,0:T(8,128)(2,1)S(1)} copy(bf16[1024,8,96]{0,2,1:T(8,128)(2,1)} %bitcast.33) | data formatting | bytes 3145728 | tf_op jit(solution)/shard_map/reshape | solution.py:54
  73.5 18.1 %fusion.26 = f32[1024,8,96]{2,1,0:T(8,128)} fusion(bf16[1024,8,96]{2,1,0:T(8,128)(2,1)S(1)} %copy.16, bf16[1024,96,96]{2,1,0:T(8,128)(2,1)} %copy.17), kind=kOutput, calls=%fused_computation.34 | convolution fusion | flops 150994944 | bytes 23592960 | tf_op jit(solution)/shard_map/kij,krj->kri/dot_general | solution.py:55
  91.6 3.9 %copy.18 = f32[1024,8,96]{0,2,1:T(8,128)S(1)} copy(f32[1024,8,96]{2,1,0:T(8,128)} %fusion.26) | data formatting | bytes 6291456 | tf_op jit(solution)/shard_map/kij,krj->kri/dot_general | solution.py:55
  95.5 36.4 %reduce-scatter.3.cloned.1.call-done = f32[64,768]{1,0:T(8,128)} async-done(((f32[1024,768]{1,0:T(8,128)}), f32[64,768]{1,0:T(8,128)}) %reduce-scatter.3.cloned.1.call-update) | async-done | bytes 196624 | tf_op jit(solution)/shard_map/reduce_scatter | solution.py:58
  131.9 3.5 %fusion = bf16[64,768]{1,0:T(8,128)(2,1)} fusion(f32[64,768]{1,0:T(8,128)} %reduce-scatter.3.cloned.1.call-done, f32[1024,768]{0,1:T(8,128)S(1)} %bitcast.28, s32[1024]{0:T(1024)S(1)} %copy-done.1), kind=kOutput, calls=%fused_computation.10 | convolution fusion | flops 604209152 | bytes 3444736 | tf_op jit(solution)/shard_map/dot_general | solution.py:18
  135.4 0.0 all-gather.5.cloned.1.call-update
  135.4 0.3 reduce-scatter.5.cloned.1.call-start
  135.7 2.8 %convolution_convert_fusion = bf16[1024,768]{0,1:T(8,128)(2,1)} fusion(bf16[64,768]{1,0:T(8,128)(2,1)} %fusion, s32[1024]{0:T(1024)S(1)} %copy-done.1), kind=kOutput, calls=%fused_computation.2 | convolution fusion | flops 101515264 | bytes 1675264 | tf_op jit(solution)/shard_map/dot_general | solution.py:14
  138.5 3.3 %copy.25 = bf16[1024,8,96]{2,1,0:T(8,128)(2,1)S(1)} copy(bf16[1024,8,96]{0,2,1:T(8,128)(2,1)} %bitcast.31) | data formatting | bytes 3145728 | tf_op jit(solution)/shard_map/reshape | solution.py:46
  141.7 13.6 %broadcast_multiply_fusion = f32[1024,8,96]{2,1,0:T(8,128)} fusion(f32[1024]{0:T(1024)S(1)} %convert_element_type.36, bf16[1024,8,96]{2,1,0:T(8,128)(2,1)S(1)} %copy.25, bf16[1024,96,96]{2,1,0:T(8,128)(2,1)} %copy.17), kind=kOutput, calls=%fused_computation | convolution fusion | flops 151781376 | bytes 23597056 | tf_op jit(solution)/shard_map/kij,kri->krj/dot_general | solution.py:48
  155.3 3.9 %copy.27 = f32[1024,8,96]{0,2,1:T(8,128)S(1)} copy(f32[1024,8,96]{2,1,0:T(8,128)} %broadcast_multiply_fusion) | data formatting | bytes 6291456 | tf_op jit(solution)/shard_map/mul | solution.py:48
  159.2 2.0 fusion.5
  161.2 3.4 %fusion.2 = f32[1024,768]{1,0:T(8,128)} fusion(f32[256,768]{1,0:T(8,128)S(1)} %fusion.5, s32[256]{0:T(256)S(1)} %add.26), kind=kOutput, calls=%fused_computation.13 | convolution fusion | flops 2416181248 | bytes 3933184 | tf_op jit(solution)/shard_map/dot_general | solution.py:18
  164.6 0.0 reduce-scatter.5.cloned.1.call-update
  164.6 10.7 %all-gather.5.cloned.1.call-done = bf16[1024,768]{1,0:T(8,128)(2,1)} async-done(((bf16[64,768]{1,0:T(8,128)(2,1)}), bf16[1024,768]{1,0:T(8,128)(2,1)}) %all-gather.5.cloned.1.call-update) | async-done | bytes 1572880 | tf_op jit(solution)/shard_map/all_gather | solution.py:52
  175.3 4.0 %convolution_convert_fusion.2 = bf16[1024,768]{0,1:T(8,128)(2,1)} fusion(bf16[1024,768]{1,0:T(8,128)(2,1)} %all-gather.5.cloned.1.call-done, s32[256]{0:T(256)S(1)} %add.26, s32[1024]{0:T(1024)S(1)} %copy-done.2), kind=kOutput, calls=%fused_computation.4 | convolution fusion | flops 806813696 | bytes 3150848 | tf_op jit(solution)/shard_map/dot_general | solution.py:14
  179.3 3.3 %copy.22 = bf16[1024,8,96]{2,1,0:T(8,128)(2,1)S(1)} copy(bf16[1024,8,96]{0,2,1:T(8,128)(2,1)} %bitcast.32) | data formatting | bytes 3145728 | tf_op jit(solution)/shard_map/reshape | solution.py:54
  182.6 18.0 %fusion.27 = f32[1024,8,96]{2,1,0:T(8,128)} fusion(bf16[1024,8,96]{2,1,0:T(8,128)(2,1)S(1)} %copy.22, bf16[1024,96,96]{2,1,0:T(8,128)(2,1)} %copy.17), kind=kOutput, calls=%fused_computation.35 | convolution fusion | flops 150994944 | bytes 23592960 | tf_op jit(solution)/shard_map/kij,krj->kri/dot_general | solution.py:55
  200.6 3.9 %copy.24 = f32[1024,8,96]{0,2,1:T(8,128)S(1)} copy(f32[1024,8,96]{2,1,0:T(8,128)} %fusion.27) | data formatting | bytes 6291456 | tf_op jit(solution)/shard_map/kij,krj->kri/dot_general | solution.py:55
  204.5 38.6 %reduce-scatter.5.cloned.1.call-done = f32[64,768]{1,0:T(8,128)} async-done(((f32[1024,768]{1,0:T(8,128)}), f32[64,768]{1,0:T(8,128)}) %reduce-scatter.5.cloned.1.call-update) | async-done | bytes 196624 | tf_op jit(solution)/shard_map/reduce_scatter | solution.py:58
  243.1 3.5 %fusion.1 = bf16[64,768]{1,0:T(8,128)(2,1)} fusion(f32[64,768]{1,0:T(8,128)} %reduce-scatter.5.cloned.1.call-done, f32[1024,768]{0,1:T(8,128)S(1)} %bitcast.29, s32[1024]{0:T(1024)S(1)} %copy-done.1), kind=kOutput, calls=%fused_computation.11 | convolution fusion | flops 604209152 | bytes 3444736 | tf_op jit(solution)/shard_map/dot_general | solution.py:18
  (3 shorter events, 0.0 us)
Async XLA Ops:
  7.2 59.0 %all-gather.3.cloned.1.call-start = ((), (), s32[]{:S(2)}) async-start(), calls=%async_computation.2 | async-start | bytes 1671168 | tf_op jit(solution)/shard_map/all_gather | solution.py:52
  7.9 29.7 %copy-start.4 = (s32[1024]{0:T(1024)S(1)}, s32[1024]{0:T(1024)}, u32[]{:S(2)}) copy-start(s32[1024]{0:T(1024)} %param.10) | copy-start | bytes 12292
  7.9 29.7 %copy-start = (bf16[64,768]{1,0:T(8,128)(2,1)S(1)}, bf16[64,768]{1,0:T(8,128)(2,1)}, u32[]{:S(2)}) copy-start(bf16[64,768]{1,0:T(8,128)(2,1)} %param.6) | copy-start | bytes 294916
  7.9 29.7 %copy-start.1 = (s32[1024]{0:T(1024)S(1)}, s32[1024]{0:T(1024)}, u32[]{:S(2)}) copy-start(s32[1024]{0:T(1024)} %param.8) | copy-start | bytes 12292
  7.9 123.9 %reduce-scatter.3.cloned.1.call-start = ((), (), s32[]{:S(2)}) async-start(), calls=%async_computation.3 | async-start | bytes 3342336 | tf_op jit(solution)/shard_map/reduce_scatter | solution.py:58
  56.4 4.1 %copy-start.3 = (s32[1,16,16]{2,1,0:T(8,128)S(1)}, s32[1,16,16]{2,1,0:T(8,128)}, u32[]{:S(2)}) copy-start(s32[1,16,16]{2,1,0:T(8,128)} %param.11) | copy-start | bytes 3076
  56.4 4.1 %copy-start.2 = (s32[1024]{0:T(1024)S(1)}, s32[1024]{0:T(1024)}, u32[]{:S(2)}) copy-start(s32[1024]{0:T(1024)} %param.9) | copy-start | bytes 12292
  65.9 109.4 %all-gather.5.cloned.1.call-start = ((), (), s32[]{:S(2)}) async-start(), calls=%async_computation.4 | async-start | bytes 1671168 | tf_op jit(solution)/shard_map/all_gather | solution.py:52
  135.4 107.7 %reduce-scatter.5.cloned.1.call-start = ((), (), s32[]{:S(2)}) async-start(), calls=%async_computation.5 | async-start | bytes 3342336 | tf_op jit(solution)/shard_map/reduce_scatter | solution.py:58
Sparse Core Ops, SparseCore 0:
  10.3 40.1 all-gather.2
  66.1 65.7 reduce-scatter.2
  135.5 39.7 all-gather.4
  179.0 64.0 reduce-scatter.4
where the time goes:
time: 258 us; the launch traced here: 253 us
  matrix products  93.8 us (36%)
  waiting for transfers between devices  86.4 us (33%)
  local copies, waits for them, and re-layouts  58.4 us (23%)
  between operations  13.9 us (5%)
    reduce_scatter x2, waiting for transfers between devices, operate(): lax.psum_scatter(dense_part, 'row', scatter_dimension=0, tiled=True)  75 us
    dot_general x2, matrix products, operate(): jnp.einsum('kij,krj->kri', tiles, far_forces, preferred_element_type=jnp....  36.1 us
    unnamed x11, local copies, waits for them, and re-layouts  29.6 us
    dot_general x2, matrix products, operate(): jnp.einsum('kij,kri->krj', tiles, own_forces, preferred_element_type=jnp....  27.1 us
    dot_general x6, matrix products, sum_rows(): lax.dot_general(table, partial_rows, (((0,), (0,)), ((), ())), precision=...  17.8 us
    dot_general x4, matrix products, pick_rows(): jnp.dot(table, values, preferred_element_type=jnp.float32)  12.8 us
    all_gather x2, waiting for transfers between devices, operate(): all_rows = lax.all_gather(current, 'row', axis=0, tiled=True)  10.7 us
    mul x2, local copies, waits for them, and re-layouts, operate(): jnp.einsum('kij,kri->krj', tiles, own_forces, preferred_element_type=jnp....  7.74 us
  transfers between devices with their start and end apart: 4, of which 3 were waited for; matrix products, arithmetic and copies ran while one was open for 57% of the time, Pallas kernels for 0%

commit v1 on v0

v1 whole, which is shorter than its diff:
```python
import functools

import jax
import jax.numpy as jnp
from jax import lax
from jax.experimental import pallas as pl
from jax.experimental.pallas import tpu as pltpu
from jax.sharding import PartitionSpec as P

NRHS = 8
BANKS = 4
UNROLL = 16
BLOCK = 128


def pass_kernel(mirrored, pick_s, put_s, flag_s, tiles_ref, table_ref, out_ref, acc_ref):
    step = pl.program_id(0)

    @pl.when(step == 0)
    def _():
        acc_ref[...] = jnp.zeros_like(acc_ref)

    base = step * BLOCK

    def group(g, carry):
        start = pl.multiple_of(g * UNROLL, UNROLL)
        products = []
        for u in range(UNROLL):
            k = base + start + u
            x = table_ref[pick_s[k]]
            tile = tiles_ref[start + u]
            if mirrored:
                x = (x.astype(jnp.float32) * flag_s[k].astype(jnp.float32)).astype(jnp.bfloat16)
                dims = (((1,), (0,)), ((), ()))
            else:
                dims = (((1,), (1,)), ((), ()))
            products.append(lax.dot_general(x, tile, dims, preferred_element_type=jnp.float32))
        for u in range(UNROLL):
            row = put_s[base + start + u]
            acc_ref[u % BANKS, row] += products[u]
        return carry

    lax.fori_loop(0, BLOCK // UNROLL, group, 0)

    @pl.when(step == pl.num_programs(0) - 1)
    def _():
        out_ref[...] = (acc_ref[0] + acc_ref[1]) + (acc_ref[2] + acc_ref[3])


def tile_pass(mirrored, pick, put, flag, tiles, table, rows):
    count, unknowns = tiles.shape[0], tiles.shape[1]
    return pl.pallas_call(
        functools.partial(pass_kernel, mirrored),
        out_shape=jax.ShapeDtypeStruct((rows, NRHS, unknowns), jnp.float32),
        grid_spec=pltpu.PrefetchScalarGridSpec(
            num_scalar_prefetch=3,
            grid=(count // BLOCK,),
            in_specs=[
                pl.BlockSpec((BLOCK, unknowns, unknowns), lambda s, *_: (s, 0, 0)),
                pl.BlockSpec(table.shape, lambda s, *_: (0, 0, 0)),
            ],
            out_specs=pl.BlockSpec((rows, NRHS, unknowns), lambda s, *_: (0, 0, 0)),
            scratch_shapes=[pltpu.VMEM((BANKS, rows, NRHS, unknowns), jnp.float32)],
        ),
        compiler_params=pltpu.CompilerParams(vmem_limit_bytes=48 * 2**20),
        cost_estimate=pl.CostEstimate(
            flops=2 * count * NRHS * unknowns * unknowns,
            bytes_accessed=2 * count * unknowns * 128,
            transcendentals=0,
        ),
        name="mirror_pass" if mirrored else "direct_pass",
    )(pick, put, flag, tiles, table)


def combine_kernel(row_s, own_ref, got_ref, out_ref, acc_ref):
    acc_ref[0] = own_ref[...]
    for b in range(1, BANKS):
        acc_ref[b] = jnp.zeros(acc_ref.shape[1:], acc_ref.dtype)

    def group(g, carry):
        start = pl.multiple_of(g * UNROLL, UNROLL)
        for u in range(UNROLL):
            acc_ref[u % BANKS, row_s[start + u]] += got_ref[start + u]
        return carry

    lax.fori_loop(0, got_ref.shape[0] // UNROLL, group, 0)
    total = (acc_ref[0] + acc_ref[1]) + (acc_ref[2] + acc_ref[3])
    out_ref[...] = total.astype(out_ref.dtype)


def combine(rows, own, got):
    vmem = pl.BlockSpec(memory_space=pltpu.VMEM)
    return pl.pallas_call(
        combine_kernel,
        out_shape=jax.ShapeDtypeStruct(own.shape, jnp.bfloat16),
        in_specs=[pl.BlockSpec(memory_space=pltpu.SMEM), vmem, vmem],
        out_specs=vmem,
        scratch_shapes=[pltpu.VMEM((BANKS,) + own.shape, jnp.float32)],
        compiler_params=pltpu.CompilerParams(vmem_limit_bytes=32 * 2**20),
        name="combine_rows",
    )(rows, own, got)


def per_device(forces, tiles, tile_local, tile_slot, tile_flag, want_list):
    peers = lax.axis_size("row")
    fibres, width = forces.shape
    unknowns = tiles.shape[1]
    capacity = want_list.shape[2]
    slots = peers * capacity
    wanted = want_list[0]
    asked = lax.all_to_all(wanted, "row", 0, 0, tiled=True).reshape(-1)
    far_table = (jnp.arange(peers, dtype=jnp.int32)[:, None] * fibres + wanted).reshape(-1)
    slot_hot = tile_slot[:, None] == jnp.arange(slots, dtype=jnp.int32)[None, :]
    far_row = jnp.sum(jnp.where(slot_hot, far_table[None, :], 0), axis=1)

    def operate(current):
        everyone = lax.all_gather(current, "row", axis=0, tiled=True)
        slot_part = tile_pass(True, tile_local, tile_slot, tile_flag, tiles, current, slots)
        got = lax.all_to_all(slot_part, "row", 0, 0, tiled=True)
        own_part = tile_pass(False, far_row, tile_local, tile_flag, tiles, everyone, fibres)
        return combine(asked, own_part, got)

    one = operate(forces.reshape(fibres, NRHS, unknowns))
    two = operate(one)
    return (one.reshape(fibres, width), two.reshape(fibres, width))


def solution(mesh):
    in_specs = (
        P(("groups", "row"), None),
        P(("groups", "row"), None, None),
        P(("groups", "row")),
        P(("groups", "row")),
        P(("groups", "row")),
        P(("groups", "row"), None, None),
    )
    out_specs = (P(("groups", "row"), None), P(("groups", "row"), None))
    return jax.shard_map(
        per_device, mesh=mesh, in_specs=in_specs, out_specs=out_specs, check_vma=False
    )
```

time: 258 us -> 191 us (0.74)
  the two profiles are of different devices: /device:TPU:9 before, /device:TPU:0 now
where the time goes in v1:
time: 191 us; the launch traced here: 189 us
  Pallas kernels  88.1 us (46%)
  local copies, waits for them, and re-layouts  38 us (20%)
  waiting for transfers between devices  28.2 us (15%)
  starting transfers between devices  19.5 us (10%)
  between operations  14.2 us (7%)
    pallas_call x4, Pallas kernels, tile_pass(): pl.pallas_call(functools.partial(pass_kernel, mirrored), out_shape=jax.Sh...  84.7 us
    unnamed x15, local copies, waits for them, and re-layouts  33 us
    all_gather x2, waiting for transfers between devices, operate(): everyone = lax.all_gather(current, 'row', axis=0, tiled=True)  28.2 us
    all_to_all x2, starting transfers between devices, operate(): got = lax.all_to_all(slot_part, 'row', 0, 0, tiled=True)  12 us
    all_to_all x1, starting transfers between devices, per_device(): asked = lax.all_to_all(wanted, 'row', 0, 0, tiled=True).reshape(-1)  7.4 us
  transfers between devices with their start and end apart: 5, of which 1 were waited for; matrix products, arithmetic and copies ran while one was open for 18% of the time, Pallas kernels for 45%

profile of v1, /device:TPU:0, one launch (start us, length us, event | category | flops | bytes accessed | tf_op | source)
XLA Modules:
  0.0 189.0 jit_solution(125333238554190317)
XLA Ops:
  7.2 0.0 all-gather.3.cloned.1.call-start
  7.2 1.7 reshape.38.table_ref
  8.9 0.0 all-gather.3.cloned.1.call-update
  8.9 7.4 %all-to-all-start = ((s32[16,1,16]{2,1,0:T(1,128)}), s32[16,1,16]{2,1,0:T(1,128)S(1)}, u32[]{:S(2)}, u32[]{:S(2)}) async-start(s32[16,1,16]{2,1,0:T(1,128)} %bitcast.1), calls=%async_computation | async-start | bytes 16384 | tf_op jit(solution)/shard_map/all_to_all | solution.py:111
  16.3 0.0 copy-start.2
  16.3 0.0 copy-start.3
  16.4 0.0 copy-start.4
  16.4 0.0 copy-start.5
  16.4 29.8 %copy.16.tiles_ref = bf16[1024,96,96]{2,1,0:T(8,128)(2,1)} copy(bf16[1024,96,96]{0,2,1:T(8,128)(2,1)} %param.7) | data formatting | bytes 37748736 | tf_op args[1]
  46.1 0.0 copy-done.2
  46.1 0.0 copy-done.3
  46.1 0.0 copy-done.4
  46.1 0.0 copy-done.5
  46.2 0.0 copy-start.6
  46.2 18.9 %mirror_pass.2 = f32[256,8,96]{2,1,0:T(8,128)} custom-call(s32[1024]{0:T(1024)S(1)} %copy-done.3, s32[1024]{0:T(1024)S(1)} %copy-done.5, s32[1024]{0:T(1024)S(1)} %copy-done.4, bf16[1024,96,96]{2,1,0:T(8,128)(2,1)} %copy.16.tiles_ref, bf16[64,8,96]{2,1,0:T(8,128)(2,1)S(1)} %copy-done.2), custom_call_target="tpu_custom_call" | custom-call | flops 150994944 | bytes 25165824 | tf_op jit(solution)/shard_map/mirror_pass/pallas_call | solution.py:52
  65.1 0.0 all-to-all-done
  65.1 6.0 %all-to-all-start.1 = ((f32[256,8,96]{2,1,0:T(8,128)}), f32[256,8,96]{2,1,0:T(8,128)S(1)}, u32[]{:S(2)}, u32[]{:S(2)}) async-start(f32[256,8,96]{2,1,0:T(8,128)} %mirror_pass.2), calls=%async_computation.1 | async-start | bytes 2097152 | tf_op jit(solution)/shard_map/all_to_all | solution.py:119
  71.1 0.0 all-gather.5.cloned.1.call-start
  71.1 0.0 copy-done.6
  71.1 0.1 squeeze.3
  71.2 0.1 add.14
  71.3 0.1 add.15
  71.4 0.4 select_reduce_fusion.pick_s
  71.7 0.5 broadcast.16
  72.3 0.7 reduce.3
  72.9 0.1 reshape.37.row_s
  73.0 0.0 all-gather.3.cloned.1.call-done.table_ref
  73.0 0.0 copy-start
  73.0 1.6 copy-done
  74.6 23.5 %direct_pass.2.own_ref = f32[64,8,96]{2,1,0:T(8,128)S(1)} custom-call(s32[1024]{0:T(1024)S(1)} %select_reduce_fusion.pick_s, s32[1024]{0:T(1024)S(1)} %copy-done.3, s32[1024]{0:T(1024)S(1)} %copy-done.4, bf16[1024,96,96]{2,1,0:T(8,128)(2,1)} %copy.16.tiles_ref, bf16[1024,8,96]{2,1,0:T(8,128)(2,1)S(1)} %copy-done), custom_call_target="tpu_custom_call" | custom-call | flops 150994944 | bytes 25165824 | tf_op jit(solution)/shard_map/direct_pass/pallas_call | solution.py:52
  98.1 0.0 all-to-all-done.1.got_ref
  98.1 2.0 %combine_rows.2.table_ref = bf16[64,8,96]{2,1,0:T(8,128)(2,1)} custom-call(s32[256]{0:T(256)S(1)} %reshape.37.row_s, f32[64,8,96]{2,1,0:T(8,128)S(1)} %direct_pass.2.own_ref, f32[256,8,96]{2,1,0:T(8,128)S(1)} %all-to-all-done.1.got_ref), custom_call_target="tpu_custom_call" | custom-call | tf_op jit(solution)/shard_map/combine_rows/pallas_call | solution.py:93
  100.1 0.0 all-gather.5.cloned.1.call-update
  100.1 18.9 %mirror_pass.3 = f32[256,8,96]{2,1,0:T(8,128)} custom-call(s32[1024]{0:T(1024)S(1)} %copy-done.3, s32[1024]{0:T(1024)S(1)} %copy-done.5, s32[1024]{0:T(1024)S(1)} %copy-done.4, bf16[1024,96,96]{2,1,0:T(8,128)(2,1)} %copy.16.tiles_ref, bf16[64,8,96]{2,1,0:T(8,128)(2,1)} %combine_rows.2.table_ref), custom_call_target="tpu_custom_call" | custom-call | flops 150994944 | bytes 25165824 | tf_op jit(solution)/shard_map/mirror_pass/pallas_call | solution.py:52
  119.0 6.0 %all-to-all-start.2 = ((f32[256,8,96]{2,1,0:T(8,128)}), f32[256,8,96]{2,1,0:T(8,128)S(1)}, u32[]{:S(2)}, u32[]{:S(2)}) async-start(f32[256,8,96]{2,1,0:T(8,128)} %mirror_pass.3), calls=%async_computation.2 | async-start | bytes 2097152 | tf_op jit(solution)/shard_map/all_to_all | solution.py:119
  125.0 1.7 reshape.39
  126.7 28.2 %all-gather.5.cloned.1.call-done.table_ref = bf16[1024,8,96]{2,1,0:T(8,128)(2,1)} async-done(((bf16[64,8,96]{2,1,0:T(8,128)(2,1)}), bf16[1024,8,96]{2,1,0:T(8,128)(2,1)}) %all-gather.5.cloned.1.call-update) | async-done | bytes 1572880 | tf_op jit(solution)/shard_map/all_gather | solution.py:117
  154.9 0.0 copy-start.1
  154.9 1.6 copy-done.1
  156.5 23.5 %direct_pass.3.own_ref = f32[64,8,96]{2,1,0:T(8,128)S(1)} custom-call(s32[1024]{0:T(1024)S(1)} %select_reduce_fusion.pick_s, s32[1024]{0:T(1024)S(1)} %copy-done.3, s32[1024]{0:T(1024)S(1)} %copy-done.4, bf16[1024,96,96]{2,1,0:T(8,128)(2,1)} %copy.16.tiles_ref, bf16[1024,8,96]{2,1,0:T(8,128)(2,1)S(1)} %copy-done.1), custom_call_target="tpu_custom_call" | custom-call | flops 150994944 | bytes 25165824 | tf_op jit(solution)/shard_map/direct_pass/pallas_call | solution.py:52
  180.0 0.0 all-to-all-done.2.got_ref
  180.0 1.4 combine_rows.3
  181.4 0.8 reshape.40
  (2 shorter events, 0.0 us)
Async XLA Ops:
  7.2 65.8 %all-gather.3.cloned.1.call-start = ((), (), s32[]{:S(2)}) async-start(), calls=%async_computation.3 | async-start | bytes 2228224 | tf_op jit(solution)/shard_map/all_gather | solution.py:117
  8.9 56.1 %all-to-all-start = ((s32[16,1,16]{2,1,0:T(1,128)}), s32[16,1,16]{2,1,0:T(1,128)S(1)}, u32[]{:S(2)}, u32[]{:S(2)}) async-start(s32[16,1,16]{2,1,0:T(1,128)} %bitcast.1), calls=%async_computation | async-start | bytes 16384 | tf_op jit(solution)/shard_map/all_to_all | solution.py:111
  16.3 29.8 %copy-start.2 = (bf16[64,8,96]{2,1,0:T(8,128)(2,1)S(1)}, bf16[64,8,96]{2,1,0:T(8,128)(2,1)}, u32[]{:S(2)}) copy-start(bf16[64,8,96]{2,1,0:T(8,128)(2,1)} %reshape.38.table_ref) | copy-start | bytes 294916
  16.3 29.8 %copy-start.3 = (s32[1024]{0:T(1024)S(1)}, s32[1024]{0:T(1024)}, u32[]{:S(2)}) copy-start(s32[1024]{0:T(1024)} %pick_s.3) | copy-start | bytes 12292
  16.4 29.8 %copy-start.4 = (s32[1024]{0:T(1024)S(1)}, s32[1024]{0:T(1024)}, u32[]{:S(2)}) copy-start(s32[1024]{0:T(1024)} %flag_s.7) | copy-start | bytes 12292
  16.4 29.8 %copy-start.5 = (s32[1024]{0:T(1024)S(1)}, s32[1024]{0:T(1024)}, u32[]{:S(2)}) copy-start(s32[1024]{0:T(1024)} %put_s.7) | copy-start | bytes 12292
  46.2 25.0 %copy-start.6 = (s32[1,16,16]{2,1,0:T(8,128)S(1)}, s32[1,16,16]{2,1,0:T(8,128)}, u32[]{:S(2)}) copy-start(s32[1,16,16]{2,1,0:T(8,128)} %param.11) | copy-start | bytes 3076
  65.1 33.0 %all-to-all-start.1 = ((f32[256,8,96]{2,1,0:T(8,128)}), f32[256,8,96]{2,1,0:T(8,128)S(1)}, u32[]{:S(2)}, u32[]{:S(2)}) async-start(f32[256,8,96]{2,1,0:T(8,128)} %mirror_pass.2), calls=%async_computation.1 | async-start | bytes 2097152 | tf_op jit(solution)/shard_map/all_to_all | solution.py:119
  71.1 83.9 %all-gather.5.cloned.1.call-start = ((), (), s32[]{:S(2)}) async-start(), calls=%async_computation.4 | async-start | bytes 2228224 | tf_op jit(solution)/shard_map/all_gather | solution.py:117
  73.0 1.6 copy-start
  119.0 61.0 %all-to-all-start.2 = ((f32[256,8,96]{2,1,0:T(8,128)}), f32[256,8,96]{2,1,0:T(8,128)S(1)}, u32[]{:S(2)}, u32[]{:S(2)}) async-start(f32[256,8,96]{2,1,0:T(8,128)} %mirror_pass.3), calls=%async_computation.2 | async-start | bytes 2097152 | tf_op jit(solution)/shard_map/all_to_all | solution.py:119
  154.9 1.6 copy-start.1
Sparse Core Ops, SparseCore 0:
  10.2 44.0 all-gather.2
  100.2 54.6 all-gather.4

commit v2 on v1

v2 whole, which is shorter than its diff:
```python
import functools

import jax
import jax.numpy as jnp
from jax import lax
from jax.experimental import pallas as pl
from jax.experimental.pallas import tpu as pltpu
from jax.sharding import PartitionSpec as P

NRHS = 8
BANKS = 4
UNROLL = 64
ROWS = 16
BLOCK = 128


def pass_kernel(mirrored, pick_s, put_s, flag_s, tiles_ref, table_ref, out_ref, near_ref, *banks):
    step = pl.program_id(0)
    unknowns = tiles_ref.shape[1]
    pair = BANKS // 2

    @pl.when(step == 0)
    def _():
        for bank in banks:
            bank[...] = jnp.zeros_like(bank)
        values = table_ref[...].astype(jnp.float32)
        if mirrored:
            blank = jnp.zeros_like(values)
            near_ref[0] = jnp.concatenate([values, blank], axis=2)
            near_ref[1] = jnp.concatenate([blank, values], axis=2)
        else:
            near_ref[0] = values

    base = step * BLOCK

    def operand(k, side):
        if mirrored:
            return near_ref[side, pick_s[k]] * flag_s[k].astype(jnp.float32)
        return near_ref[0, pick_s[k]]

    def group(g, carry):
        start = pl.multiple_of(g * UNROLL, UNROLL)
        for u in range(0, UNROLL, 2):
            k = base + start + u
            both = jnp.concatenate([operand(k, 0), operand(k + 1, 1)], axis=0).astype(jnp.bfloat16)
            stacked = tiles_ref[pl.ds(start + u, 2)].reshape(2 * unknowns, unknowns)
            dims = (((1,), (0 if mirrored else 1,)), ((), ()))
            product = lax.dot_general(both, stacked, dims, preferred_element_type=jnp.float32)
            which = (u // 2) % pair
            banks[2 * which][put_s[k]] += product[:NRHS, :unknowns]
            banks[2 * which + 1][put_s[k + 1]] += product[NRHS:]
        return carry

    lax.fori_loop(0, BLOCK // UNROLL, group, 0)

    @pl.when(step == pl.num_programs(0) - 1)
    def _():
        even, odd = banks[0][...], banks[1][...]
        for which in range(1, pair):
            even += banks[2 * which][...]
            odd += banks[2 * which + 1][...]
        out_ref[...] = even + odd[:, :, odd.shape[2] - unknowns:]


def tile_pass(mirrored, pick, put, flag, tiles, table, rows):
    count, unknowns = tiles.shape[0], tiles.shape[1]
    near = pltpu.VMEM(
        (2, table.shape[0], NRHS, 2 * unknowns) if mirrored else (1,) + table.shape, jnp.float32
    )
    return pl.pallas_call(
        functools.partial(pass_kernel, mirrored),
        out_shape=jax.ShapeDtypeStruct((rows, NRHS, unknowns), jnp.float32),
        grid_spec=pltpu.PrefetchScalarGridSpec(
            num_scalar_prefetch=3,
            grid=(count // BLOCK,),
            in_specs=[
                pl.BlockSpec((BLOCK, unknowns, unknowns), lambda s, *_: (s, 0, 0)),
                pl.BlockSpec(table.shape, lambda s, *_: (0, 0, 0)),
            ],
            out_specs=pl.BlockSpec((rows, NRHS, unknowns), lambda s, *_: (0, 0, 0)),
            scratch_shapes=[near]
            + [
                pltpu.VMEM((rows, NRHS, unknowns * (1 if mirrored or b % 2 == 0 else 2)), jnp.float32)
                for b in range(BANKS)
            ],
        ),
        compiler_params=pltpu.CompilerParams(vmem_limit_bytes=48 * 2**20),
        cost_estimate=pl.CostEstimate(
            flops=2 * count * NRHS * unknowns * unknowns,
            bytes_accessed=2 * count * unknowns * 128,
            transcendentals=0,
        ),
        name="mirror_pass" if mirrored else "direct_pass",
    )(pick, put, flag, tiles, table)


def gather_kernel(row_s, from_ref, out_ref, wide_ref):
    wide_ref[...] = from_ref[...].astype(jnp.float32)
    send_rows(row_s, wide_ref, out_ref)


def send_rows(row_s, wide_ref, out_ref):
    def group(g, carry):
        start = pl.multiple_of(g * ROWS, ROWS)
        for u in range(ROWS):
            out_ref[start + u] = wide_ref[row_s[start + u]].astype(out_ref.dtype)
        return carry

    lax.fori_loop(0, out_ref.shape[0] // ROWS, group, 0)


def gather(rows, table):
    vmem = pl.BlockSpec(memory_space=pltpu.VMEM)
    return pl.pallas_call(
        gather_kernel,
        out_shape=jax.ShapeDtypeStruct(rows.shape + table.shape[1:], jnp.bfloat16),
        in_specs=[pl.BlockSpec(memory_space=pltpu.SMEM), vmem],
        out_specs=vmem,
        scratch_shapes=[pltpu.VMEM(table.shape, jnp.float32)],
        compiler_params=pltpu.CompilerParams(vmem_limit_bytes=32 * 2**20),
        name="gather_rows",
    )(rows, table)


def combine_kernel(row_s, own_ref, got_ref, out_ref, *rest):
    banks = rest[-BANKS:]
    banks[0][...] = own_ref[...]
    for bank in banks[1:]:
        bank[...] = jnp.zeros_like(bank)

    def group(g, carry):
        start = pl.multiple_of(g * ROWS, ROWS)
        for u in range(ROWS):
            banks[u % BANKS][row_s[start + u]] += got_ref[start + u]
        return carry

    lax.fori_loop(0, got_ref.shape[0] // ROWS, group, 0)
    total = banks[0][...]
    for bank in banks[1:]:
        total += bank[...]
    out_ref[...] = total.astype(out_ref.dtype)
    if len(rest) > BANKS:
        banks[0][...] = total
        send_rows(row_s, banks[0], rest[0])


def combine(rows, own, got, send):
    vmem = pl.BlockSpec(memory_space=pltpu.VMEM)
    out = [jax.ShapeDtypeStruct(own.shape, jnp.bfloat16)]
    if send:
        out.append(jax.ShapeDtypeStruct(got.shape, jnp.bfloat16))
    return pl.pallas_call(
        combine_kernel,
        out_shape=out,
        in_specs=[pl.BlockSpec(memory_space=pltpu.SMEM), vmem, vmem],
        out_specs=[vmem] * len(out),
        scratch_shapes=[pltpu.VMEM(own.shape, jnp.float32)] * BANKS,
        compiler_params=pltpu.CompilerParams(vmem_limit_bytes=32 * 2**20),
        name="combine_rows",
    )(rows, own, got)


def per_device(forces, tiles, tile_local, tile_slot, tile_flag, want_list):
    peers = lax.axis_size("row")
    fibres, width = forces.shape
    unknowns = tiles.shape[1]
    capacity = want_list.shape[2]
    slots = peers * capacity
    wanted = want_list[0]
    asked = lax.all_to_all(wanted, "row", 0, 0, tiled=True).reshape(-1)
    def operate(current, sent, again):
        far = lax.all_to_all(sent, "row", 0, 0, tiled=True)
        slot_part = tile_pass(True, tile_local, tile_slot, tile_flag, tiles, current, slots)
        got = lax.all_to_all(slot_part, "row", 0, 0, tiled=True)
        own_part = tile_pass(False, tile_slot, tile_local, tile_flag, tiles, far, fibres)
        return combine(asked, own_part, got, again)

    start = forces.reshape(fibres, NRHS, unknowns)
    one, sent = operate(start, gather(asked, start), True)
    (two,) = operate(one, sent, False)
    return (one.reshape(fibres, width), two.reshape(fibres, width))


def solution(mesh):
    in_specs = (
        P(("groups", "row"), None),
        P(("groups", "row"), None, None),
        P(("groups", "row")),
        P(("groups", "row")),
        P(("groups", "row")),
        P(("groups", "row"), None, None),
    )
    out_specs = (P(("groups", "row"), None), P(("groups", "row"), None))
    return jax.shard_map(
        per_device, mesh=mesh, in_specs=in_specs, out_specs=out_specs, check_vma=False
    )
```

time: 191 us -> 154 us (0.81)
  the two profiles are of different devices: /device:TPU:0 before, /device:TPU:9 now
where the time goes in v2:
time: 154 us; the launch traced here: 152 us
  Pallas kernels  72.6 us (47%)
  local copies, waits for them, and re-layouts  32.8 us (21%)
  starting transfers between devices  29 us (19%)
  waiting for transfers between devices  16.3 us (11%)
    pallas_call x4, Pallas kernels, tile_pass(): pl.pallas_call(functools.partial(pass_kernel, mirrored), out_shape=jax.Sh...  67.6 us
    unnamed x7, local copies, waits for them, and re-layouts  29.6 us
    all_to_all x2, waiting for transfers between devices, operate(): got = lax.all_to_all(slot_part, 'row', 0, 0, tiled=True)  12.8 us
    all_to_all x2, starting transfers between devices, operate(): got = lax.all_to_all(slot_part, 'row', 0, 0, tiled=True)  12.1 us
    all_to_all x2, starting transfers between devices, operate(): far = lax.all_to_all(sent, 'row', 0, 0, tiled=True)  10.2 us
    all_to_all x1, starting transfers between devices, per_device(): asked = lax.all_to_all(wanted, 'row', 0, 0, tiled=True).reshape(-1)  6.75 us
    all_to_all x1, waiting for transfers between devices, per_device(): asked = lax.all_to_all(wanted, 'row', 0, 0, tiled=True).reshape(-1)  3.56 us
    pallas_call x2, Pallas kernels, combine(): pl.pallas_call(combine_kernel, out_shape=out, in_specs=[pl.BlockSpec(memo...  3.27 us
  transfers between devices with their start and end apart: 5, of which 3 were waited for; matrix products, arithmetic and copies ran while one was open for 21% of the time, Pallas kernels for 44%

profile of v2, /device:TPU:9, one launch (start us, length us, event | category | flops | bytes accessed | tf_op | source)
XLA Modules:
  0.0 152.1 jit_solution(6655267385991154303)
XLA Ops:
  0.6 0.0 copy-start.2
  0.6 0.0 copy-start
  0.7 0.0 copy-start.1
  0.7 6.8 %all-to-all-start = ((s32[16,1,16]{2,1,0:T(1,128)}), s32[16,1,16]{2,1,0:T(1,128)S(1)}, u32[]{:S(2)}, u32[]{:S(2)}) async-start(s32[16,1,16]{2,1,0:T(1,128)} %bitcast.1), calls=%async_computation | async-start | bytes 16384 | tf_op jit(solution)/shard_map/all_to_all | solution.py:170
  7.4 1.0 reshape.21.from_ref.table_ref
  8.5 3.6 %all-to-all-done = s32[16,1,16]{2,1,0:T(1,128)S(1)} async-done(((s32[16,1,16]{2,1,0:T(1,128)}), s32[16,1,16]{2,1,0:T(1,128)S(1)}, u32[]{:S(2)}, u32[]{:S(2)}) %all-to-all-start) | async-done | bytes 1056 | tf_op jit(solution)/shard_map/all_to_all | solution.py:170
  12.0 0.5 broadcast.3
  12.5 0.7 reduce.3
  13.2 0.1 reshape.20.row_s
  13.3 1.7 %gather_rows.1 = bf16[256,8,96]{2,1,0:T(8,128)(2,1)} custom-call(s32[256]{0:T(256)S(1)} %reshape.20.row_s, bf16[64,8,96]{2,1,0:T(8,128)(2,1)S(1)} %reshape.21.from_ref.table_ref), custom_call_target="tpu_custom_call" | custom-call | tf_op jit(solution)/shard_map/gather_rows/pallas_call | solution.py:114
  15.0 5.2 %all-to-all-start.1 = ((bf16[256,8,96]{2,1,0:T(8,128)(2,1)}), bf16[256,8,96]{2,1,0:T(8,128)(2,1)S(1)}, u32[]{:S(2)}, u32[]{:S(2)}) async-start(bf16[256,8,96]{2,1,0:T(8,128)(2,1)} %gather_rows.1), calls=%async_computation.1 | async-start | bytes 1048576 | tf_op jit(solution)/shard_map/all_to_all | solution.py:172
  20.2 29.6 %copy.12.tiles_ref = bf16[1024,96,96]{2,1,0:T(8,128)(2,1)} copy(bf16[1024,96,96]{0,2,1:T(8,128)(2,1)} %param.7) | data formatting | bytes 37748736 | tf_op args[1]
  49.8 0.0 copy-done.2
  49.8 0.0 copy-done
  49.8 0.0 copy-done.1
  49.8 15.7 %mirror_pass.2 = f32[256,8,96]{2,1,0:T(8,128)} custom-call(s32[1024]{0:T(1024)S(1)} %copy-done.1, s32[1024]{0:T(1024)S(1)} %copy-done, s32[1024]{0:T(1024)S(1)} %copy-done.2, bf16[1024,96,96]{2,1,0:T(8,128)(2,1)} %copy.12.tiles_ref, bf16[64,8,96]{2,1,0:T(8,128)(2,1)S(1)} %reshape.21.from_ref.table_ref), custom_call_target="tpu_custom_call" | custom-call | flops 150994944 | bytes 25165824 | tf_op jit(solution)/shard_map/mirror_pass/pallas_call | solution.py:70
  65.6 0.0 all-to-all-done.1.table_ref
  65.6 6.1 %all-to-all-start.2 = ((f32[256,8,96]{2,1,0:T(8,128)}), f32[256,8,96]{2,1,0:T(8,128)S(1)}, u32[]{:S(2)}, u32[]{:S(2)}) async-start(f32[256,8,96]{2,1,0:T(8,128)} %mirror_pass.2), calls=%async_computation.2 | async-start | bytes 2097152 | tf_op jit(solution)/shard_map/all_to_all | solution.py:174
  71.7 18.1 %direct_pass.2.own_ref = f32[64,8,96]{2,1,0:T(8,128)S(1)} custom-call(s32[1024]{0:T(1024)S(1)} %copy-done, s32[1024]{0:T(1024)S(1)} %copy-done.1, s32[1024]{0:T(1024)S(1)} %copy-done.2, bf16[1024,96,96]{2,1,0:T(8,128)(2,1)} %copy.12.tiles_ref, bf16[256,8,96]{2,1,0:T(8,128)(2,1)S(1)} %all-to-all-done.1.table_ref), custom_call_target="tpu_custom_call" | custom-call | flops 150994944 | bytes 25165824 | tf_op jit(solution)/shard_map/direct_pass/pallas_call | solution.py:70
  89.7 6.8 %all-to-all-done.2.got_ref = f32[256,8,96]{2,1,0:T(8,128)S(1)} async-done(((f32[256,8,96]{2,1,0:T(8,128)}), f32[256,8,96]{2,1,0:T(8,128)S(1)}, u32[]{:S(2)}, u32[]{:S(2)}) %all-to-all-start.2) | async-done | bytes 786464 | tf_op jit(solution)/shard_map/all_to_all | solution.py:174
  96.5 2.2 %combine_rows.2 = (bf16[64,8,96]{2,1,0:T(8,128)(2,1)S(1)}, bf16[256,8,96]{2,1,0:T(8,128)(2,1)}) custom-call(s32[256]{0:T(256)S(1)} %reshape.20.row_s, f32[64,8,96]{2,1,0:T(8,128)S(1)} %direct_pass.2.own_ref, f32[256,8,96]{2,1,0:T(8,128)S(1)} %all-to-all-done.2.got_ref), custom_call_target="tpu_custom_call" | custom-call | tf_op jit(solution)/shard_map/combine_rows/pallas_call | solution.py:152
  98.7 5.0 %all-to-all-start.3 = ((bf16[256,8,96]{2,1,0:T(8,128)(2,1)}), bf16[256,8,96]{2,1,0:T(8,128)(2,1)S(1)}, u32[]{:S(2)}, u32[]{:S(2)}) async-start(bf16[256,8,96]{2,1,0:T(8,128)(2,1)} %get-tuple-element.5), calls=%async_computation.3 | async-start | bytes 1048576 | tf_op jit(solution)/shard_map/all_to_all | solution.py:172
  103.7 15.7 %mirror_pass.3 = f32[256,8,96]{2,1,0:T(8,128)} custom-call(s32[1024]{0:T(1024)S(1)} %copy-done.1, s32[1024]{0:T(1024)S(1)} %copy-done, s32[1024]{0:T(1024)S(1)} %copy-done.2, bf16[1024,96,96]{2,1,0:T(8,128)(2,1)} %copy.12.tiles_ref, bf16[64,8,96]{2,1,0:T(8,128)(2,1)S(1)} %get-tuple-element.4.table_ref), custom_call_target="tpu_custom_call" | custom-call | flops 150994944 | bytes 25165824 | tf_op jit(solution)/shard_map/mirror_pass/pallas_call | solution.py:70
  119.4 0.0 all-to-all-done.3.table_ref
  119.4 6.0 %all-to-all-start.4 = ((f32[256,8,96]{2,1,0:T(8,128)}), f32[256,8,96]{2,1,0:T(8,128)S(1)}, u32[]{:S(2)}, u32[]{:S(2)}) async-start(f32[256,8,96]{2,1,0:T(8,128)} %mirror_pass.3), calls=%async_computation.4 | async-start | bytes 2097152 | tf_op jit(solution)/shard_map/all_to_all | solution.py:174
  125.5 0.8 reshape.22
  126.2 18.1 %direct_pass.3.own_ref = f32[64,8,96]{2,1,0:T(8,128)S(1)} custom-call(s32[1024]{0:T(1024)S(1)} %copy-done, s32[1024]{0:T(1024)S(1)} %copy-done.1, s32[1024]{0:T(1024)S(1)} %copy-done.2, bf16[1024,96,96]{2,1,0:T(8,128)(2,1)} %copy.12.tiles_ref, bf16[256,8,96]{2,1,0:T(8,128)(2,1)S(1)} %all-to-all-done.3.table_ref), custom_call_target="tpu_custom_call" | custom-call | flops 150994944 | bytes 25165824 | tf_op jit(solution)/shard_map/direct_pass/pallas_call | solution.py:70
  144.3 6.0 %all-to-all-done.4.got_ref = f32[256,8,96]{2,1,0:T(8,128)S(1)} async-done(((f32[256,8,96]{2,1,0:T(8,128)}), f32[256,8,96]{2,1,0:T(8,128)S(1)}, u32[]{:S(2)}, u32[]{:S(2)}) %all-to-all-start.4) | async-done | bytes 786464 | tf_op jit(solution)/shard_map/all_to_all | solution.py:174
  150.3 1.0 combine_rows.3
  151.4 0.8 reshape.23
Async XLA Ops:
  0.6 49.2 %copy-start.2 = (s32[1024]{0:T(1024)S(1)}, s32[1024]{0:T(1024)}, u32[]{:S(2)}) copy-start(s32[1024]{0:T(1024)} %flag_s.7) | copy-start | bytes 12292
  0.6 49.2 %copy-start = (s32[1024]{0:T(1024)S(1)}, s32[1024]{0:T(1024)}, u32[]{:S(2)}) copy-start(s32[1024]{0:T(1024)} %put_s.7) | copy-start | bytes 12292
  0.7 49.2 %copy-start.1 = (s32[1024]{0:T(1024)S(1)}, s32[1024]{0:T(1024)}, u32[]{:S(2)}) copy-start(s32[1024]{0:T(1024)} %pick_s.7) | copy-start | bytes 12292
  0.7 11.4 %all-to-all-start = ((s32[16,1,16]{2,1,0:T(1,128)}), s32[16,1,16]{2,1,0:T(1,128)S(1)}, u32[]{:S(2)}, u32[]{:S(2)}) async-start(s32[16,1,16]{2,1,0:T(1,128)} %bitcast.1), calls=%async_computation | async-start | bytes 16384 | tf_op jit(solution)/shard_map/all_to_all | solution.py:170
  15.0 50.5 %all-to-all-start.1 = ((bf16[256,8,96]{2,1,0:T(8,128)(2,1)}), bf16[256,8,96]{2,1,0:T(8,128)(2,1)S(1)}, u32[]{:S(2)}, u32[]{:S(2)}) async-start(bf16[256,8,96]{2,1,0:T(8,128)(2,1)} %gather_rows.1), calls=%async_computation.1 | async-start | bytes 1048576 | tf_op jit(solution)/shard_map/all_to_all | solution.py:172
  65.6 30.9 %all-to-all-start.2 = ((f32[256,8,96]{2,1,0:T(8,128)}), f32[256,8,96]{2,1,0:T(8,128)S(1)}, u32[]{:S(2)}, u32[]{:S(2)}) async-start(f32[256,8,96]{2,1,0:T(8,128)} %mirror_pass.2), calls=%async_computation.2 | async-start | bytes 2097152 | tf_op jit(solution)/shard_map/all_to_all | solution.py:174
  98.7 20.7 %all-to-all-start.3 = ((bf16[256,8,96]{2,1,0:T(8,128)(2,1)}), bf16[256,8,96]{2,1,0:T(8,128)(2,1)S(1)}, u32[]{:S(2)}, u32[]{:S(2)}) async-start(bf16[256,8,96]{2,1,0:T(8,128)(2,1)} %get-tuple-element.5), calls=%async_computation.3 | async-start | bytes 1048576 | tf_op jit(solution)/shard_map/all_to_all | solution.py:172
  119.4 30.9 %all-to-all-start.4 = ((f32[256,8,96]{2,1,0:T(8,128)}), f32[256,8,96]{2,1,0:T(8,128)S(1)}, u32[]{:S(2)}, u32[]{:S(2)}) async-start(f32[256,8,96]{2,1,0:T(8,128)} %mirror_pass.3), calls=%async_computation.4 | async-start | bytes 2097152 | tf_op jit(solution)/shard_map/all_to_all | solution.py:174

commit v3 on v2

--- a/solution.py
+++ b/solution.py
@@ -10,14 +10,55 @@
 NRHS = 8
 BANKS = 4
 UNROLL = 64
+LANES = 128
 ROWS = 16
 BLOCK = 128
 
 
-def pass_kernel(mirrored, pick_s, put_s, flag_s, tiles_ref, table_ref, out_ref, near_ref, *banks):
+def pair_kernel(tiles_ref, out_ref, turned_ref):
+    unknowns = tiles_ref.shape[0]
+    half = BLOCK // 2
+    blank = jnp.zeros((LANES - unknowns, BLOCK), tiles_ref.dtype)
+
+    def turn(g, carry):
+        for u in range(8):
+            i = g * 8 + u
+            turned = jnp.concatenate([tiles_ref[i], blank], axis=0).T
+            turned_ref[pl.ds(pl.multiple_of(i * BLOCK, BLOCK), BLOCK), :] = turned.astype(jnp.float32)
+        return carry
+
+    lax.fori_loop(0, unknowns // 8, turn, 0)
+
+    def place(g, carry):
+        for u in range(4):
+            p = g * 4 + u
+            low = turned_ref[pl.ds(p, unknowns, stride=BLOCK), :]
+            high = turned_ref[pl.ds(p + half, unknowns, stride=BLOCK), :]
+            out_ref[p] = jnp.concatenate([low, high], axis=1).astype(out_ref.dtype)
+        return carry
+
+    lax.fori_loop(0, half // 4, place, 0)
+
+
+def pair_tiles(tiles):
+    count, unknowns = tiles.shape[0], tiles.shape[1]
+    return pl.pallas_call(
+        pair_kernel,
+        out_shape=jax.ShapeDtypeStruct((count // 2, unknowns, 2 * LANES), tiles.dtype),
+        grid=(count // BLOCK,),
+        in_specs=[pl.BlockSpec((unknowns, unknowns, BLOCK), lambda s: (0, 0, s))],
+        out_specs=pl.BlockSpec((BLOCK // 2, unknowns, 2 * LANES), lambda s: (s, 0, 0)),
+        scratch_shapes=[pltpu.VMEM((unknowns * BLOCK, LANES), jnp.float32)],
+        compiler_params=pltpu.CompilerParams(vmem_limit_bytes=48 * 2**20),
+        cost_estimate=pl.CostEstimate(flops=0, bytes_accessed=44 * 2**20, transcendentals=0),
+        name="pair_tiles",
+    )(jnp.transpose(tiles, (1, 2, 0)))
+
+
+def pass_kernel(mirrored, pick_s, put_s, flag_s, pairs_ref, table_ref, out_ref, near_ref, *banks):
     step = pl.program_id(0)
-    unknowns = tiles_ref.shape[1]
-    pair = BANKS // 2
+    unknowns = pairs_ref.shape[1]
+    half = BLOCK // 2
 
     @pl.when(step == 0)
     def _():
@@ -29,44 +70,53 @@
             near_ref[0] = jnp.concatenate([values, blank], axis=2)
             near_ref[1] = jnp.concatenate([blank, values], axis=2)
         else:
-            near_ref[0] = values
+            blank = jnp.zeros(values.shape[:2] + (LANES - unknowns,), jnp.float32)
+            near_ref[0] = jnp.concatenate([values, blank], axis=2)
 
     base = step * BLOCK
-
-    def operand(k, side):
+    empty = jnp.zeros((NRHS, LANES), jnp.float32)
+
+    def operand(k, place):
         if mirrored:
-            return near_ref[side, pick_s[k]] * flag_s[k].astype(jnp.float32)
-        return near_ref[0, pick_s[k]]
+            return near_ref[place // 2, pick_s[k]] * flag_s[k].astype(jnp.float32)
+        x = near_ref[0, pick_s[k]]
+        return jnp.concatenate([empty, x] if place % 2 else [x, empty], axis=1)
 
     def group(g, carry):
-        start = pl.multiple_of(g * UNROLL, UNROLL)
-        for u in range(0, UNROLL, 2):
+        start = pl.multiple_of(g * (UNROLL // 2), UNROLL // 2)
+        for u in range(0, UNROLL // 2, 2):
             k = base + start + u
-            both = jnp.concatenate([operand(k, 0), operand(k + 1, 1)], axis=0).astype(jnp.bfloat16)
-            stacked = tiles_ref[pl.ds(start + u, 2)].reshape(2 * unknowns, unknowns)
+            members = (k, k + half, k + 1, k + 1 + half)
+            rows = jnp.concatenate([operand(m, n) for n, m in enumerate(members)], axis=0)
+            stacked = pairs_ref[pl.ds(start + u, 2)].reshape(2 * unknowns, 2 * LANES)
             dims = (((1,), (0 if mirrored else 1,)), ((), ()))
-            product = lax.dot_general(both, stacked, dims, preferred_element_type=jnp.float32)
-            which = (u // 2) % pair
-            banks[2 * which][put_s[k]] += product[:NRHS, :unknowns]
-            banks[2 * which + 1][put_s[k + 1]] += product[NRHS:]
+            product = lax.dot_general(
+                rows.astype(jnp.bfloat16), stacked, dims, preferred_element_type=jnp.float32
+            )
+            for n, m in enumerate(members):
+                part = product[n * NRHS:(n + 1) * NRHS]
+                if mirrored:
+                    part = part[:, (n % 2) * LANES:(n % 2 + 1) * LANES]
+                else:
+                    part = part[:, :banks[n].shape[2]]
+                banks[n][put_s[m]] += part
         return carry
 
     lax.fori_loop(0, BLOCK // UNROLL, group, 0)
 
     @pl.when(step == pl.num_programs(0) - 1)
     def _():
-        even, odd = banks[0][...], banks[1][...]
-        for which in range(1, pair):
-            even += banks[2 * which][...]
-            odd += banks[2 * which + 1][...]
-        out_ref[...] = even + odd[:, :, odd.shape[2] - unknowns:]
-
-
-def tile_pass(mirrored, pick, put, flag, tiles, table, rows):
-    count, unknowns = tiles.shape[0], tiles.shape[1]
-    near = pltpu.VMEM(
-        (2, table.shape[0], NRHS, 2 * unknowns) if mirrored else (1,) + table.shape, jnp.float32
-    )
+        low, high = banks[0][...] + banks[1][...], banks[2][...] + banks[3][...]
+        if mirrored:
+            out_ref[...] = (low + high)[:, :, :unknowns]
+        else:
+            out_ref[...] = low[:, :, :unknowns] + high[:, :, unknowns:]
+
+
+def tile_pass(mirrored, pick, put, flag, pairs, table, rows):
+    count, unknowns = 2 * pairs.shape[0], pairs.shape[1]
+    near = (2, table.shape[0], NRHS, 2 * unknowns) if mirrored else (1, table.shape[0], NRHS, LANES)
+    widths = (LANES,) * BANKS if mirrored else (LANES, LANES, 2 * unknowns, 2 * unknowns)
     return pl.pallas_call(
         functools.partial(pass_kernel, mirrored),
         out_shape=jax.ShapeDtypeStruct((rows, NRHS, unknowns), jnp.float32),
@@ -74,24 +124,21 @@
             num_scalar_prefetch=3,
             grid=(count // BLOCK,),
             in_specs=[
-                pl.BlockSpec((BLOCK, unknowns, unknowns), lambda s, *_: (s, 0, 0)),
+                pl.BlockSpec((BLOCK // 2, unknowns, 2 * LANES), lambda s, *_: (s, 0, 0)),
                 pl.BlockSpec(table.shape, lambda s, *_: (0, 0, 0)),
             ],
             out_specs=pl.BlockSpec((rows, NRHS, unknowns), lambda s, *_: (0, 0, 0)),
-            scratch_shapes=[near]
-            + [
-                pltpu.VMEM((rows, NRHS, unknowns * (1 if mirrored or b % 2 == 0 else 2)), jnp.float32)
-                for b in range(BANKS)
-            ],
+            scratch_shapes=[pltpu.VMEM(near, jnp.float32)]
+            + [pltpu.VMEM((rows, NRHS, width), jnp.float32) for width in widths],
         ),
         compiler_params=pltpu.CompilerParams(vmem_limit_bytes=48 * 2**20),
         cost_estimate=pl.CostEstimate(
             flops=2 * count * NRHS * unknowns * unknowns,
-            bytes_accessed=2 * count * unknowns * 128,
+            bytes_accessed=2 * count * unknowns * LANES,
             transcendentals=0,
         ),
         name="mirror_pass" if mirrored else "direct_pass",
-    )(pick, put, flag, tiles, table)
+    )(pick, put, flag, pairs, table)
 
 
 def gather_kernel(row_s, from_ref, out_ref, wide_ref):
@@ -167,12 +214,14 @@
     capacity = want_list.shape[2]
     slots = peers * capacity
     wanted = want_list[0]
-    asked = lax.all_to_all(wanted, "row", 0, 0, tiled=True).reshape(-1)
+    everyone = lax.all_gather(wanted, "row", axis=0)
+    asked = lax.dynamic_index_in_dim(everyone, lax.axis_index("row"), 1, False).reshape(-1)
+    pairs = pair_tiles(tiles)
     def operate(current, sent, again):
         far = lax.all_to_all(sent, "row", 0, 0, tiled=True)
-        slot_part = tile_pass(True, tile_local, tile_slot, tile_flag, tiles, current, slots)
+        slot_part = tile_pass(True, tile_local, tile_slot, tile_flag, pairs, current, slots)
         got = lax.all_to_all(slot_part, "row", 0, 0, tiled=True)
-        own_part = tile_pass(False, tile_slot, tile_local, tile_flag, tiles, far, fibres)
+        own_part = tile_pass(False, tile_slot, tile_local, tile_flag, pairs, far, fibres)
         return combine(asked, own_part, got, again)
 
     start = forces.reshape(fibres, NRHS, unknowns)

time: 154 us -> 193 us (1.25)
  Pallas kernels: 72.6 us -> 127 us
  local copies, waits for them, and re-layouts: 32.8 us -> 2.75 us
  blocking collectives: 0 us -> 19.9 us
  starting transfers between devices: 29 us -> 23.5 us
  waiting for transfers between devices: 16.3 us -> 18.6 us
    pallas_call x0 -> x1, Pallas kernels: none -> 61.6 us  [pair_tiles(): pl.pallas_call(pair_kernel, out_shape=jax.ShapeDtypeStruct((count // 2, u...]
    unnamed x7 -> x6, local copies, waits for them, and re-layouts: 29.6 us -> 0.01 us
    all_gather x0 -> x1, blocking collectives: none -> 19.9 us  [per_device(): everyone = lax.all_gather(wanted, 'row', axis=0)]
    pallas_call x4, Pallas kernels: 67.6 us -> 60 us  [tile_pass(): pl.pallas_call(functools.partial(pass_kernel, mirrored), out_shape=jax.Sh...]
    all_to_all x1 -> x0, starting transfers between devices: 6.75 us -> none  [per_device(): asked = lax.all_to_all(wanted, 'row', 0, 0, tiled=True).reshape(-1)]
    all_to_all x2, waiting for transfers between devices: 12.8 us -> 18.6 us  [operate(): got = lax.all_to_all(slot_part, 'row', 0, 0, tiled=True)]
    all_to_all x1 -> x0, waiting for transfers between devices: 3.56 us -> none  [per_device(): asked = lax.all_to_all(wanted, 'row', 0, 0, tiled=True).reshape(-1)]
  transfers between devices with their start and end apart: 5 -> 4, of which waited for: 3 -> 2; matrix products, arithmetic and copies ran while one was open for 21% -> 0% of each run, Pallas kernels for 44% -> 63%
where the time goes in v3:
time: 193 us; the launch traced here: 192 us
  Pallas kernels  127 us (66%)
  starting transfers between devices  23.5 us (12%)
  blocking collectives  19.9 us (10%)
  waiting for transfers between devices  18.6 us (10%)
  local copies, waits for them, and re-layouts  2.75 us (1%)
    pallas_call x1, Pallas kernels, pair_tiles(): pl.pallas_call(pair_kernel, out_shape=jax.ShapeDtypeStruct((count // 2, u...  61.6 us
    pallas_call x4, Pallas kernels, tile_pass(): pl.pallas_call(functools.partial(pass_kernel, mirrored), out_shape=jax.Sh...  60 us
    all_gather x1, blocking collectives, per_device(): everyone = lax.all_gather(wanted, 'row', axis=0)  19.9 us
    all_to_all x2, waiting for transfers between devices, operate(): got = lax.all_to_all(slot_part, 'row', 0, 0, tiled=True)  18.6 us
    all_to_all x2, starting transfers between devices, operate(): got = lax.all_to_all(slot_part, 'row', 0, 0, tiled=True)  12.1 us
    all_to_all x2, starting transfers between devices, operate(): far = lax.all_to_all(sent, 'row', 0, 0, tiled=True)  11.4 us
  transfers between devices with their start and end apart: 4, of which 2 were waited for; matrix products, arithmetic and copies ran while one was open for 0% of the time, Pallas kernels for 63%

profile of v3, /device:TPU:9, one launch (start us, length us, event | category | flops | bytes accessed | tf_op | source)
XLA Modules:
  0.0 192.1 jit_solution(435092175198476868)
XLA Ops:
  0.6 0.0 copy-start.2
  0.6 0.0 copy-start
  0.7 0.0 copy-start.1
  0.7 1.1 reshape.18.from_ref.table_ref
  1.7 19.9 %all_gather.3 = s32[16,16,16]{2,1,0:T(8,128)S(1)} all-gather(s32[1,16,16]{2,1,0:T(8,128)} %param.11), channel_id=1, replica_groups=mesh['groups'=2,'row'=16] {'row'}, dimensions={0}, use_global_device_ids=true | all-gather | bytes 17408 | tf_op jit(solution)/shard_map/all_gather | solution.py:217
  21.7 0.1 reshape.17.row_s
  21.8 1.7 gather_rows.1
  23.5 6.4 %all-to-all-start = ((bf16[256,8,96]{2,1,0:T(8,128)(2,1)}), bf16[256,8,96]{2,1,0:T(8,128)(2,1)S(1)}, u32[]{:S(2)}, u32[]{:S(2)}) async-start(bf16[256,8,96]{2,1,0:T(8,128)(2,1)} %gather_rows.1), calls=%async_computation | async-start | bytes 1048576 | tf_op jit(solution)/shard_map/all_to_all | solution.py:221
  30.0 61.6 %pair_tiles.1.pairs_ref = bf16[512,96,256]{2,1,0:T(8,128)(2,1)} custom-call(bf16[96,96,1024]{2,1,0:T(8,128)(2,1)} %bitcast.1), custom_call_target="tpu_custom_call" | custom-call | bytes 46137344 | tf_op jit(solution)/shard_map/pair_tiles/pallas_call | solution.py:45
  91.6 0.0 copy-done.2
  91.6 0.0 copy-done
  91.6 0.0 copy-done.1
  91.6 14.8 %mirror_pass.2 = f32[256,8,96]{2,1,0:T(8,128)} custom-call(s32[1024]{0:T(1024)S(1)} %copy-done.1, s32[1024]{0:T(1024)S(1)} %copy-done, s32[1024]{0:T(1024)S(1)} %copy-done.2, bf16[512,96,256]{2,1,0:T(8,128)(2,1)} %pair_tiles.1.pairs_ref, bf16[64,8,96]{2,1,0:T(8,128)(2,1)S(1)} %reshape.18.from_ref.table_ref), custom_call_target="tpu_custom_call" | custom-call | flops 150994944 | bytes 25165824 | tf_op jit(solution)/shard_map/mirror_pass/pallas_call | solution.py:120
  106.5 0.0 all-to-all-done.table_ref
  106.5 6.1 %all-to-all-start.1 = ((f32[256,8,96]{2,1,0:T(8,128)}), f32[256,8,96]{2,1,0:T(8,128)S(1)}, u32[]{:S(2)}, u32[]{:S(2)}) async-start(f32[256,8,96]{2,1,0:T(8,128)} %mirror_pass.2), calls=%async_computation.1 | async-start | bytes 2097152 | tf_op jit(solution)/shard_map/all_to_all | solution.py:223
  112.5 15.2 %direct_pass.2.own_ref = f32[64,8,96]{2,1,0:T(8,128)S(1)} custom-call(s32[1024]{0:T(1024)S(1)} %copy-done, s32[1024]{0:T(1024)S(1)} %copy-done.1, s32[1024]{0:T(1024)S(1)} %copy-done.2, bf16[512,96,256]{2,1,0:T(8,128)(2,1)} %pair_tiles.1.pairs_ref, bf16[256,8,96]{2,1,0:T(8,128)(2,1)S(1)} %all-to-all-done.table_ref), custom_call_target="tpu_custom_call" | custom-call | flops 150994944 | bytes 25165824 | tf_op jit(solution)/shard_map/direct_pass/pallas_call | solution.py:120
  127.7 9.7 %all-to-all-done.1.got_ref = f32[256,8,96]{2,1,0:T(8,128)S(1)} async-done(((f32[256,8,96]{2,1,0:T(8,128)}), f32[256,8,96]{2,1,0:T(8,128)S(1)}, u32[]{:S(2)}, u32[]{:S(2)}) %all-to-all-start.1) | async-done | bytes 786464 | tf_op jit(solution)/shard_map/all_to_all | solution.py:223
  137.4 2.2 %combine_rows.2 = (bf16[64,8,96]{2,1,0:T(8,128)(2,1)S(1)}, bf16[256,8,96]{2,1,0:T(8,128)(2,1)}) custom-call(s32[256]{0:T(256)S(1)} %reshape.17.row_s, f32[64,8,96]{2,1,0:T(8,128)S(1)} %direct_pass.2.own_ref, f32[256,8,96]{2,1,0:T(8,128)S(1)} %all-to-all-done.1.got_ref), custom_call_target="tpu_custom_call" | custom-call | tf_op jit(solution)/shard_map/combine_rows/pallas_call | solution.py:199
  139.6 5.0 %all-to-all-start.2 = ((bf16[256,8,96]{2,1,0:T(8,128)(2,1)}), bf16[256,8,96]{2,1,0:T(8,128)(2,1)S(1)}, u32[]{:S(2)}, u32[]{:S(2)}) async-start(bf16[256,8,96]{2,1,0:T(8,128)(2,1)} %get-tuple-element.5), calls=%async_computation.2 | async-start | bytes 1048576 | tf_op jit(solution)/shard_map/all_to_all | solution.py:221
  144.6 14.8 %mirror_pass.3 = f32[256,8,96]{2,1,0:T(8,128)} custom-call(s32[1024]{0:T(1024)S(1)} %copy-done.1, s32[1024]{0:T(1024)S(1)} %copy-done, s32[1024]{0:T(1024)S(1)} %copy-done.2, bf16[512,96,256]{2,1,0:T(8,128)(2,1)} %pair_tiles.1.pairs_ref, bf16[64,8,96]{2,1,0:T(8,128)(2,1)S(1)} %get-tuple-element.4.table_ref), custom_call_target="tpu_custom_call" | custom-call | flops 150994944 | bytes 25165824 | tf_op jit(solution)/shard_map/mirror_pass/pallas_call | solution.py:120
  159.4 0.0 all-to-all-done.2.table_ref
  159.4 6.0 %all-to-all-start.3 = ((f32[256,8,96]{2,1,0:T(8,128)}), f32[256,8,96]{2,1,0:T(8,128)S(1)}, u32[]{:S(2)}, u32[]{:S(2)}) async-start(f32[256,8,96]{2,1,0:T(8,128)} %mirror_pass.3), calls=%async_computation.3 | async-start | bytes 2097152 | tf_op jit(solution)/shard_map/all_to_all | solution.py:223
  165.4 0.8 reshape.19
  166.2 15.2 %direct_pass.3.own_ref = f32[64,8,96]{2,1,0:T(8,128)S(1)} custom-call(s32[1024]{0:T(1024)S(1)} %copy-done, s32[1024]{0:T(1024)S(1)} %copy-done.1, s32[1024]{0:T(1024)S(1)} %copy-done.2, bf16[512,96,256]{2,1,0:T(8,128)(2,1)} %pair_tiles.1.pairs_ref, bf16[256,8,96]{2,1,0:T(8,128)(2,1)S(1)} %all-to-all-done.2.table_ref), custom_call_target="tpu_custom_call" | custom-call | flops 150994944 | bytes 25165824 | tf_op jit(solution)/shard_map/direct_pass/pallas_call | solution.py:120
  181.4 8.9 %all-to-all-done.3.got_ref = f32[256,8,96]{2,1,0:T(8,128)S(1)} async-done(((f32[256,8,96]{2,1,0:T(8,128)}), f32[256,8,96]{2,1,0:T(8,128)S(1)}, u32[]{:S(2)}, u32[]{:S(2)}) %all-to-all-start.3) | async-done | bytes 786464 | tf_op jit(solution)/shard_map/all_to_all | solution.py:223
  190.3 1.0 combine_rows.3
  191.3 0.8 reshape.20
  (1 shorter events, 0.0 us)
Async XLA Ops:
  0.6 91.0 %copy-start.2 = (s32[1024]{0:T(1024)S(1)}, s32[1024]{0:T(1024)}, u32[]{:S(2)}) copy-start(s32[1024]{0:T(1024)} %flag_s.7) | copy-start | bytes 12292
  0.6 91.0 %copy-start = (s32[1024]{0:T(1024)S(1)}, s32[1024]{0:T(1024)}, u32[]{:S(2)}) copy-start(s32[1024]{0:T(1024)} %put_s.7) | copy-start | bytes 12292
  0.7 91.0 %copy-start.1 = (s32[1024]{0:T(1024)S(1)}, s32[1024]{0:T(1024)}, u32[]{:S(2)}) copy-start(s32[1024]{0:T(1024)} %pick_s.7) | copy-start | bytes 12292
  23.5 82.9 %all-to-all-start = ((bf16[256,8,96]{2,1,0:T(8,128)(2,1)}), bf16[256,8,96]{2,1,0:T(8,128)(2,1)S(1)}, u32[]{:S(2)}, u32[]{:S(2)}) async-start(bf16[256,8,96]{2,1,0:T(8,128)(2,1)} %gather_rows.1), calls=%async_computation | async-start | bytes 1048576 | tf_op jit(solution)/shard_map/all_to_all | solution.py:221
  106.5 30.9 %all-to-all-start.1 = ((f32[256,8,96]{2,1,0:T(8,128)}), f32[256,8,96]{2,1,0:T(8,128)S(1)}, u32[]{:S(2)}, u32[]{:S(2)}) async-start(f32[256,8,96]{2,1,0:T(8,128)} %mirror_pass.2), calls=%async_computation.1 | async-start | bytes 2097152 | tf_op jit(solution)/shard_map/all_to_all | solution.py:223
  139.6 19.8 %all-to-all-start.2 = ((bf16[256,8,96]{2,1,0:T(8,128)(2,1)}), bf16[256,8,96]{2,1,0:T(8,128)(2,1)S(1)}, u32[]{:S(2)}, u32[]{:S(2)}) async-start(bf16[256,8,96]{2,1,0:T(8,128)(2,1)} %get-tuple-element.5), calls=%async_computation.2 | async-start | bytes 1048576 | tf_op jit(solution)/shard_map/all_to_all | solution.py:221
  159.4 30.9 %all-to-all-start.3 = ((f32[256,8,96]{2,1,0:T(8,128)}), f32[256,8,96]{2,1,0:T(8,128)S(1)}, u32[]{:S(2)}, u32[]{:S(2)}) async-start(f32[256,8,96]{2,1,0:T(8,128)} %mirror_pass.3), calls=%async_computation.3 | async-start | bytes 2097152 | tf_op jit(solution)/shard_map/all_to_all | solution.py:223

commit v4 on v3

--- a/solution.py
+++ b/solution.py
@@ -13,6 +13,7 @@
 LANES = 128
 ROWS = 16
 BLOCK = 128
+PITCH = BLOCK + 8
 
 
 def pair_kernel(tiles_ref, out_ref, turned_ref):
@@ -24,7 +25,7 @@
         for u in range(8):
             i = g * 8 + u
             turned = jnp.concatenate([tiles_ref[i], blank], axis=0).T
-            turned_ref[pl.ds(pl.multiple_of(i * BLOCK, BLOCK), BLOCK), :] = turned.astype(jnp.float32)
+            turned_ref[pl.ds(pl.multiple_of(i * PITCH, 8), BLOCK), :] = turned.astype(jnp.float32)
         return carry
 
     lax.fori_loop(0, unknowns // 8, turn, 0)
@@ -32,8 +33,8 @@
     def place(g, carry):
         for u in range(4):
             p = g * 4 + u
-            low = turned_ref[pl.ds(p, unknowns, stride=BLOCK), :]
-            high = turned_ref[pl.ds(p + half, unknowns, stride=BLOCK), :]
+            low = turned_ref[pl.ds(p, unknowns, stride=PITCH), :]
+            high = turned_ref[pl.ds(p + half, unknowns, stride=PITCH), :]
             out_ref[p] = jnp.concatenate([low, high], axis=1).astype(out_ref.dtype)
         return carry
 
@@ -48,7 +49,7 @@
         grid=(count // BLOCK,),
         in_specs=[pl.BlockSpec((unknowns, unknowns, BLOCK), lambda s: (0, 0, s))],
         out_specs=pl.BlockSpec((BLOCK // 2, unknowns, 2 * LANES), lambda s: (s, 0, 0)),
-        scratch_shapes=[pltpu.VMEM((unknowns * BLOCK, LANES), jnp.float32)],
+        scratch_shapes=[pltpu.VMEM((unknowns * PITCH, LANES), jnp.float32)],
         compiler_params=pltpu.CompilerParams(vmem_limit_bytes=48 * 2**20),
         cost_estimate=pl.CostEstimate(flops=0, bytes_accessed=44 * 2**20, transcendentals=0),
         name="pair_tiles",
@@ -214,9 +215,9 @@
     capacity = want_list.shape[2]
     slots = peers * capacity
     wanted = want_list[0]
-    everyone = lax.all_gather(wanted, "row", axis=0)
-    asked = lax.dynamic_index_in_dim(everyone, lax.axis_index("row"), 1, False).reshape(-1)
-    pairs = pair_tiles(tiles)
+    asked = lax.all_to_all(wanted, "row", 0, 0, tiled=True)
+    asked, pairs = lax.optimization_barrier((asked, pair_tiles(tiles)))
+    asked = asked.reshape(-1)
     def operate(current, sent, again):
         far = lax.all_to_all(sent, "row", 0, 0, tiled=True)
         slot_part = tile_pass(True, tile_local, tile_slot, tile_flag, pairs, current, slots)

time: 193 us -> 143 us (0.74)
  Pallas kernels: 127 us -> 90.3 us
  blocking collectives: 19.9 us -> 0 us
  starting transfers between devices: 23.5 us -> 29.8 us
    pallas_call x1, Pallas kernels: 61.6 us -> 25.3 us  [pair_tiles(): pl.pallas_call(pair_kernel, out_shape=jax.ShapeDtypeStruct((count // 2, u...]
    all_gather x1 -> x0, blocking collectives: 19.9 us -> none  [per_device(): everyone = lax.all_gather(wanted, 'row', axis=0)]
    all_to_all x0 -> x1, starting transfers between devices: none -> 6.75 us  [per_device(): asked = lax.all_to_all(wanted, 'row', 0, 0, tiled=True)]
  transfers between devices with their start and end apart: 4 -> 5, of which waited for: 2 -> 2; matrix products, arithmetic and copies ran while one was open for 0% -> 1% of each run, Pallas kernels for 63% -> 60%
where the time goes in v4:
time: 143 us; the launch traced here: 142 us
  Pallas kernels  90.3 us (63%)
  starting transfers between devices  29.8 us (21%)
  waiting for transfers between devices  18.6 us (13%)
  local copies, waits for them, and re-layouts  2.71 us (2%)
    pallas_call x4, Pallas kernels, tile_pass(): pl.pallas_call(functools.partial(pass_kernel, mirrored), out_shape=jax.Sh...  60 us
    pallas_call x1, Pallas kernels, pair_tiles(): pl.pallas_call(pair_kernel, out_shape=jax.ShapeDtypeStruct((count // 2, u...  25.3 us
    all_to_all x2, waiting for transfers between devices, operate(): got = lax.all_to_all(slot_part, 'row', 0, 0, tiled=True)  18.6 us
    all_to_all x2, starting transfers between devices, operate(): got = lax.all_to_all(slot_part, 'row', 0, 0, tiled=True)  12 us
    all_to_all x2, starting transfers between devices, operate(): far = lax.all_to_all(sent, 'row', 0, 0, tiled=True)  11 us
    all_to_all x1, starting transfers between devices, per_device(): asked = lax.all_to_all(wanted, 'row', 0, 0, tiled=True)  6.75 us
    pallas_call x2, Pallas kernels, combine(): pl.pallas_call(combine_kernel, out_shape=out, in_specs=[pl.BlockSpec(memo...  3.27 us
  transfers between devices with their start and end apart: 5, of which 2 were waited for; matrix products, arithmetic and copies ran while one was open for 1% of the time, Pallas kernels for 60%

profile of v4, /device:TPU:9, one launch (start us, length us, event | category | flops | bytes accessed | tf_op | source)
XLA Modules:
  0.0 142.1 jit_solution(3276928924272599242)
XLA Ops:
  0.6 0.0 copy-start.2
  0.6 0.0 copy-start
  0.7 0.0 copy-start.1
  0.7 6.8 %all-to-all-start = ((s32[16,1,16]{2,1,0:T(1,128)}), s32[16,1,16]{2,1,0:T(1,128)S(1)}, u32[]{:S(2)}, u32[]{:S(2)}) async-start(s32[16,1,16]{2,1,0:T(1,128)} %bitcast.5), calls=%async_computation | async-start | bytes 16384 | tf_op jit(solution)/shard_map/all_to_all | solution.py:218
  7.4 1.0 reshape.20.from_ref.table_ref
  8.5 25.3 %pair_tiles.1.pairs_ref = bf16[512,96,256]{2,1,0:T(8,128)(2,1)} custom-call(bf16[96,96,1024]{2,1,0:T(8,128)(2,1)} %bitcast.3), custom_call_target="tpu_custom_call" | custom-call | bytes 46137344 | tf_op jit(solution)/shard_map/pair_tiles/pallas_call | solution.py:46
  33.8 0.0 all-to-all-done
  33.8 0.1 reshape.19.row_s
  33.8 1.7 %gather_rows.1 = bf16[256,8,96]{2,1,0:T(8,128)(2,1)} custom-call(s32[256]{0:T(256)S(1)} %reshape.19.row_s, bf16[64,8,96]{2,1,0:T(8,128)(2,1)S(1)} %reshape.20.from_ref.table_ref), custom_call_target="tpu_custom_call" | custom-call | tf_op jit(solution)/shard_map/gather_rows/pallas_call | solution.py:162
  35.6 6.0 %all-to-all-start.1 = ((bf16[256,8,96]{2,1,0:T(8,128)(2,1)}), bf16[256,8,96]{2,1,0:T(8,128)(2,1)S(1)}, u32[]{:S(2)}, u32[]{:S(2)}) async-start(bf16[256,8,96]{2,1,0:T(8,128)(2,1)} %gather_rows.1), calls=%async_computation.1 | async-start | bytes 1048576 | tf_op jit(solution)/shard_map/all_to_all | solution.py:222
  41.6 0.0 copy-done.2
  41.6 0.0 copy-done
  41.6 0.0 copy-done.1
  41.6 14.9 %mirror_pass.2 = f32[256,8,96]{2,1,0:T(8,128)} custom-call(s32[1024]{0:T(1024)S(1)} %copy-done.1, s32[1024]{0:T(1024)S(1)} %copy-done, s32[1024]{0:T(1024)S(1)} %copy-done.2, bf16[512,96,256]{2,1,0:T(8,128)(2,1)} %pair_tiles.1.pairs_ref, bf16[64,8,96]{2,1,0:T(8,128)(2,1)S(1)} %reshape.20.from_ref.table_ref), custom_call_target="tpu_custom_call" | custom-call | flops 150994944 | bytes 25165824 | tf_op jit(solution)/shard_map/mirror_pass/pallas_call | solution.py:121
  56.5 0.0 all-to-all-done.1.table_ref
  56.5 6.0 %all-to-all-start.2 = ((f32[256,8,96]{2,1,0:T(8,128)}), f32[256,8,96]{2,1,0:T(8,128)S(1)}, u32[]{:S(2)}, u32[]{:S(2)}) async-start(f32[256,8,96]{2,1,0:T(8,128)} %mirror_pass.2), calls=%async_computation.2 | async-start | bytes 2097152 | tf_op jit(solution)/shard_map/all_to_all | solution.py:224
  62.5 15.2 %direct_pass.2.own_ref = f32[64,8,96]{2,1,0:T(8,128)S(1)} custom-call(s32[1024]{0:T(1024)S(1)} %copy-done, s32[1024]{0:T(1024)S(1)} %copy-done.1, s32[1024]{0:T(1024)S(1)} %copy-done.2, bf16[512,96,256]{2,1,0:T(8,128)(2,1)} %pair_tiles.1.pairs_ref, bf16[256,8,96]{2,1,0:T(8,128)(2,1)S(1)} %all-to-all-done.1.table_ref), custom_call_target="tpu_custom_call" | custom-call | flops 150994944 | bytes 25165824 | tf_op jit(solution)/shard_map/direct_pass/pallas_call | solution.py:121
  77.7 9.7 %all-to-all-done.2.got_ref = f32[256,8,96]{2,1,0:T(8,128)S(1)} async-done(((f32[256,8,96]{2,1,0:T(8,128)}), f32[256,8,96]{2,1,0:T(8,128)S(1)}, u32[]{:S(2)}, u32[]{:S(2)}) %all-to-all-start.2) | async-done | bytes 786464 | tf_op jit(solution)/shard_map/all_to_all | solution.py:224
  87.3 2.2 %combine_rows.2 = (bf16[64,8,96]{2,1,0:T(8,128)(2,1)S(1)}, bf16[256,8,96]{2,1,0:T(8,128)(2,1)}) custom-call(s32[256]{0:T(256)S(1)} %reshape.19.row_s, f32[64,8,96]{2,1,0:T(8,128)S(1)} %direct_pass.2.own_ref, f32[256,8,96]{2,1,0:T(8,128)S(1)} %all-to-all-done.2.got_ref), custom_call_target="tpu_custom_call" | custom-call | tf_op jit(solution)/shard_map/combine_rows/pallas_call | solution.py:200
  89.6 5.0 %all-to-all-start.3 = ((bf16[256,8,96]{2,1,0:T(8,128)(2,1)}), bf16[256,8,96]{2,1,0:T(8,128)(2,1)S(1)}, u32[]{:S(2)}, u32[]{:S(2)}) async-start(bf16[256,8,96]{2,1,0:T(8,128)(2,1)} %get-tuple-element.9), calls=%async_computation.3 | async-start | bytes 1048576 | tf_op jit(solution)/shard_map/all_to_all | solution.py:222
  94.5 14.9 %mirror_pass.3 = f32[256,8,96]{2,1,0:T(8,128)} custom-call(s32[1024]{0:T(1024)S(1)} %copy-done.1, s32[1024]{0:T(1024)S(1)} %copy-done, s32[1024]{0:T(1024)S(1)} %copy-done.2, bf16[512,96,256]{2,1,0:T(8,128)(2,1)} %pair_tiles.1.pairs_ref, bf16[64,8,96]{2,1,0:T(8,128)(2,1)S(1)} %get-tuple-element.8.table_ref), custom_call_target="tpu_custom_call" | custom-call | flops 150994944 | bytes 25165824 | tf_op jit(solution)/shard_map/mirror_pass/pallas_call | solution.py:121
  109.4 0.0 all-to-all-done.3.table_ref
  109.4 6.0 %all-to-all-start.4 = ((f32[256,8,96]{2,1,0:T(8,128)}), f32[256,8,96]{2,1,0:T(8,128)S(1)}, u32[]{:S(2)}, u32[]{:S(2)}) async-start(f32[256,8,96]{2,1,0:T(8,128)} %mirror_pass.3), calls=%async_computation.4 | async-start | bytes 2097152 | tf_op jit(solution)/shard_map/all_to_all | solution.py:224
  115.4 0.8 reshape.21
  116.2 15.2 %direct_pass.3.own_ref = f32[64,8,96]{2,1,0:T(8,128)S(1)} custom-call(s32[1024]{0:T(1024)S(1)} %copy-done, s32[1024]{0:T(1024)S(1)} %copy-done.1, s32[1024]{0:T(1024)S(1)} %copy-done.2, bf16[512,96,256]{2,1,0:T(8,128)(2,1)} %pair_tiles.1.pairs_ref, bf16[256,8,96]{2,1,0:T(8,128)(2,1)S(1)} %all-to-all-done.3.table_ref), custom_call_target="tpu_custom_call" | custom-call | flops 150994944 | bytes 25165824 | tf_op jit(solution)/shard_map/direct_pass/pallas_call | solution.py:121
  131.4 8.9 %all-to-all-done.4.got_ref = f32[256,8,96]{2,1,0:T(8,128)S(1)} async-done(((f32[256,8,96]{2,1,0:T(8,128)}), f32[256,8,96]{2,1,0:T(8,128)S(1)}, u32[]{:S(2)}, u32[]{:S(2)}) %all-to-all-start.4) | async-done | bytes 786464 | tf_op jit(solution)/shard_map/all_to_all | solution.py:224
  140.3 1.0 combine_rows.3
  141.3 0.8 reshape.22
Async XLA Ops:
  0.6 41.0 %copy-start.2 = (s32[1024]{0:T(1024)S(1)}, s32[1024]{0:T(1024)}, u32[]{:S(2)}) copy-start(s32[1024]{0:T(1024)} %flag_s.7) | copy-start | bytes 12292
  0.6 41.0 %copy-start = (s32[1024]{0:T(1024)S(1)}, s32[1024]{0:T(1024)}, u32[]{:S(2)}) copy-start(s32[1024]{0:T(1024)} %put_s.7) | copy-start | bytes 12292
  0.7 41.0 %copy-start.1 = (s32[1024]{0:T(1024)S(1)}, s32[1024]{0:T(1024)}, u32[]{:S(2)}) copy-start(s32[1024]{0:T(1024)} %pick_s.7) | copy-start | bytes 12292
  0.7 33.1 %all-to-all-start = ((s32[16,1,16]{2,1,0:T(1,128)}), s32[16,1,16]{2,1,0:T(1,128)S(1)}, u32[]{:S(2)}, u32[]{:S(2)}) async-start(s32[16,1,16]{2,1,0:T(1,128)} %bitcast.5), calls=%async_computation | async-start | bytes 16384 | tf_op jit(solution)/shard_map/all_to_all | solution.py:218
  35.6 20.9 %all-to-all-start.1 = ((bf16[256,8,96]{2,1,0:T(8,128)(2,1)}), bf16[256,8,96]{2,1,0:T(8,128)(2,1)S(1)}, u32[]{:S(2)}, u32[]{:S(2)}) async-start(bf16[256,8,96]{2,1,0:T(8,128)(2,1)} %gather_rows.1), calls=%async_computation.1 | async-start | bytes 1048576 | tf_op jit(solution)/shard_map/all_to_all | solution.py:222
  56.5 30.9 %all-to-all-start.2 = ((f32[256,8,96]{2,1,0:T(8,128)}), f32[256,8,96]{2,1,0:T(8,128)S(1)}, u32[]{:S(2)}, u32[]{:S(2)}) async-start(f32[256,8,96]{2,1,0:T(8,128)} %mirror_pass.2), calls=%async_computation.2 | async-start | bytes 2097152 | tf_op jit(solution)/shard_map/all_to_all | solution.py:224
  89.6 19.8 %all-to-all-start.3 = ((bf16[256,8,96]{2,1,0:T(8,128)(2,1)}), bf16[256,8,96]{2,1,0:T(8,128)(2,1)S(1)}, u32[]{:S(2)}, u32[]{:S(2)}) async-start(bf16[256,8,96]{2,1,0:T(8,128)(2,1)} %get-tuple-element.9), calls=%async_computation.3 | async-start | bytes 1048576 | tf_op jit(solution)/shard_map/all_to_all | solution.py:222
  109.4 30.9 %all-to-all-start.4 = ((f32[256,8,96]{2,1,0:T(8,128)}), f32[256,8,96]{2,1,0:T(8,128)S(1)}, u32[]{:S(2)}, u32[]{:S(2)}) async-start(f32[256,8,96]{2,1,0:T(8,128)} %mirror_pass.3), calls=%async_computation.4 | async-start | bytes 2097152 | tf_op jit(solution)/shard_map/all_to_all | solution.py:224

commit v5 on v4

--- a/solution.py
+++ b/solution.py
@@ -56,7 +56,27 @@
     )(jnp.transpose(tiles, (1, 2, 0)))
 
 
-def pass_kernel(mirrored, pick_s, put_s, flag_s, pairs_ref, table_ref, out_ref, near_ref, *banks):
+def pack_slots(banks, out_ref, unknowns, capacity):
+    piece = LANES - unknowns
+    share = unknowns // piece
+    kept = capacity * share // (share + 1)
+
+    def peer(p, carry):
+        rows = pl.ds(p * capacity, capacity)
+        total = (banks[0][rows] + banks[1][rows]) + (banks[2][rows] + banks[3][rows])
+        spread = [
+            total[kept + m // share][:, (m % share) * piece:(m % share + 1) * piece]
+            for m in range(kept)
+        ]
+        out_ref[pl.ds(p * kept, kept)] = jnp.concatenate(
+            [total[:kept, :, :unknowns], jnp.stack(spread)], axis=2
+        )
+        return carry
+
+    lax.fori_loop(0, out_ref.shape[0] // kept, peer, 0)
+
+
+def pass_kernel(mirrored, capacity, pick_s, put_s, flag_s, pairs_ref, table_ref, out_ref, near_ref, *banks):
     step = pl.program_id(0)
     unknowns = pairs_ref.shape[1]
     half = BLOCK // 2
@@ -107,20 +127,24 @@
 
     @pl.when(step == pl.num_programs(0) - 1)
     def _():
-        low, high = banks[0][...] + banks[1][...], banks[2][...] + banks[3][...]
         if mirrored:
-            out_ref[...] = (low + high)[:, :, :unknowns]
+            pack_slots(banks, out_ref, unknowns, capacity)
         else:
+            low, high = banks[0][...] + banks[1][...], banks[2][...] + banks[3][...]
             out_ref[...] = low[:, :, :unknowns] + high[:, :, unknowns:]
 
 
-def tile_pass(mirrored, pick, put, flag, pairs, table, rows):
+def tile_pass(mirrored, pick, put, flag, pairs, table, rows, capacity):
     count, unknowns = 2 * pairs.shape[0], pairs.shape[1]
     near = (2, table.shape[0], NRHS, 2 * unknowns) if mirrored else (1, table.shape[0], NRHS, LANES)
     widths = (LANES,) * BANKS if mirrored else (LANES, LANES, 2 * unknowns, 2 * unknowns)
-    return pl.pallas_call(
-        functools.partial(pass_kernel, mirrored),
-        out_shape=jax.ShapeDtypeStruct((rows, NRHS, unknowns), jnp.float32),
+    if mirrored:
+        out = (rows * unknowns // LANES, NRHS, LANES)
+    else:
+        out = (rows, NRHS, unknowns)
+    return pl.pallas_call(
+        functools.partial(pass_kernel, mirrored, capacity),
+        out_shape=jax.ShapeDtypeStruct(out, jnp.float32),
         grid_spec=pltpu.PrefetchScalarGridSpec(
             num_scalar_prefetch=3,
             grid=(count // BLOCK,),
@@ -128,7 +152,7 @@
                 pl.BlockSpec((BLOCK // 2, unknowns, 2 * LANES), lambda s, *_: (s, 0, 0)),
                 pl.BlockSpec(table.shape, lambda s, *_: (0, 0, 0)),
             ],
-            out_specs=pl.BlockSpec((rows, NRHS, unknowns), lambda s, *_: (0, 0, 0)),
+            out_specs=pl.BlockSpec(out, lambda s, *_: (0, 0, 0)),
             scratch_shapes=[pltpu.VMEM(near, jnp.float32)]
             + [pltpu.VMEM((rows, NRHS, width), jnp.float32) for width in widths],
         ),
@@ -170,19 +194,28 @@
     )(rows, table)
 
 
-def combine_kernel(row_s, own_ref, got_ref, out_ref, *rest):
+def combine_kernel(capacity, row_s, own_ref, got_ref, out_ref, *rest):
     banks = rest[-BANKS:]
     banks[0][...] = own_ref[...]
     for bank in banks[1:]:
         bank[...] = jnp.zeros_like(bank)
 
-    def group(g, carry):
-        start = pl.multiple_of(g * ROWS, ROWS)
-        for u in range(ROWS):
-            banks[u % BANKS][row_s[start + u]] += got_ref[start + u]
-        return carry
-
-    lax.fori_loop(0, got_ref.shape[0] // ROWS, group, 0)
+    unknowns = own_ref.shape[2]
+    piece = LANES - unknowns
+    share = unknowns // piece
+    kept = capacity * share // (share + 1)
+
+    def peer(p, carry):
+        for c in range(capacity):
+            if c < kept:
+                got = got_ref[p * kept + c][:, :unknowns]
+            else:
+                first = p * kept + (c - kept) * share
+                got = jnp.concatenate([got_ref[first + t][:, unknowns:] for t in range(share)], axis=1)
+            banks[c % BANKS][row_s[p * capacity + c]] += got
+        return carry
+
+    lax.fori_loop(0, got_ref.shape[0] // kept, peer, 0)
     total = banks[0][...]
     for bank in banks[1:]:
         total += bank[...]
@@ -192,13 +225,13 @@
         send_rows(row_s, banks[0], rest[0])
 
 
-def combine(rows, own, got, send):
+def combine(rows, own, got, capacity, send):
     vmem = pl.BlockSpec(memory_space=pltpu.VMEM)
     out = [jax.ShapeDtypeStruct(own.shape, jnp.bfloat16)]
     if send:
-        out.append(jax.ShapeDtypeStruct(got.shape, jnp.bfloat16))
-    return pl.pallas_call(
-        combine_kernel,
+        out.append(jax.ShapeDtypeStruct(rows.shape + own.shape[1:], jnp.bfloat16))
+    return pl.pallas_call(
+        functools.partial(combine_kernel, capacity),
         out_shape=out,
         in_specs=[pl.BlockSpec(memory_space=pltpu.SMEM), vmem, vmem],
         out_specs=[vmem] * len(out),
@@ -220,10 +253,10 @@
     asked = asked.reshape(-1)
     def operate(current, sent, again):
         far = lax.all_to_all(sent, "row", 0, 0, tiled=True)
-        slot_part = tile_pass(True, tile_local, tile_slot, tile_flag, pairs, current, slots)
+        slot_part = tile_pass(True, tile_local, tile_slot, tile_flag, pairs, current, slots, capacity)
         got = lax.all_to_all(slot_part, "row", 0, 0, tiled=True)
-        own_part = tile_pass(False, tile_slot, tile_local, tile_flag, pairs, far, fibres)
-        return combine(asked, own_part, got, again)
+        own_part = tile_pass(False, tile_slot, tile_local, tile_flag, pairs, far, fibres, capacity)
+        return combine(asked, own_part, got, capacity, again)
 
     start = forces.reshape(fibres, NRHS, unknowns)
     one, sent = operate(start, gather(asked, start), True)

time: 143 us -> 139 us (0.972)
  waiting for transfers between devices: 18.6 us -> 7.98 us
  Pallas kernels: 90.3 us -> 96.3 us
    all_to_all x2, waiting for transfers between devices: 18.6 us -> 7.98 us  [operate(): got = lax.all_to_all(slot_part, 'row', 0, 0, tiled=True)]
    pallas_call x6, Pallas kernels: 63.3 us -> 69.3 us  [the longest x4 64.2 us: tile_pass(): pl.pallas_call(functools.partial(pass_kernel, mirrored, capacity), out_sh...]
  transfers between devices with their start and end apart: 5 -> 5, of which waited for: 2 -> 2; matrix products, arithmetic and copies ran while one was open for 1% -> 1% of each run, Pallas kernels for 60% -> 65%
where the time goes in v5:
time: 139 us; the launch traced here: 137 us
  Pallas kernels  96.3 us (69%)
  starting transfers between devices  29.4 us (21%)
  waiting for transfers between devices  7.98 us (6%)
  local copies, waits for them, and re-layouts  2.71 us (2%)
    pallas_call x4, Pallas kernels, tile_pass(): pl.pallas_call(functools.partial(pass_kernel, mirrored, capacity), out_sh...  64.2 us
    pallas_call x1, Pallas kernels, pair_tiles(): pl.pallas_call(pair_kernel, out_shape=jax.ShapeDtypeStruct((count // 2, u...  25.3 us
    all_to_all x2, starting transfers between devices, operate(): got = lax.all_to_all(slot_part, 'row', 0, 0, tiled=True)  12 us
    all_to_all x2, starting transfers between devices, operate(): far = lax.all_to_all(sent, 'row', 0, 0, tiled=True)  10.7 us
    all_to_all x2, waiting for transfers between devices, operate(): got = lax.all_to_all(slot_part, 'row', 0, 0, tiled=True)  7.98 us
    all_to_all x1, starting transfers between devices, per_device(): asked = lax.all_to_all(wanted, 'row', 0, 0, tiled=True)  6.75 us
    pallas_call x2, Pallas kernels, combine(): pl.pallas_call(functools.partial(combine_kernel, capacity), out_shape=out...  5.08 us
  transfers between devices with their start and end apart: 5, of which 2 were waited for; matrix products, arithmetic and copies ran while one was open for 1% of the time, Pallas kernels for 65%

profile of v5, /device:TPU:9, one launch (start us, length us, event | category | flops | bytes accessed | tf_op | source)
XLA Modules:
  0.0 137.1 jit_solution(12649872767218031635)
XLA Ops:
  0.6 0.0 copy-start.2
  0.6 0.0 copy-start
  0.7 0.0 copy-start.1
  0.7 6.8 %all-to-all-start = ((s32[16,1,16]{2,1,0:T(1,128)}), s32[16,1,16]{2,1,0:T(1,128)S(1)}, u32[]{:S(2)}, u32[]{:S(2)}) async-start(s32[16,1,16]{2,1,0:T(1,128)} %bitcast.5), calls=%async_computation | async-start | bytes 16384 | tf_op jit(solution)/shard_map/all_to_all | solution.py:251
  7.4 1.0 reshape.20.from_ref.table_ref
  8.5 25.3 %pair_tiles.1.pairs_ref = bf16[512,96,256]{2,1,0:T(8,128)(2,1)} custom-call(bf16[96,96,1024]{2,1,0:T(8,128)(2,1)} %bitcast.3), custom_call_target="tpu_custom_call" | custom-call | bytes 46137344 | tf_op jit(solution)/shard_map/pair_tiles/pallas_call | solution.py:46
  33.8 0.0 all-to-all-done
  33.8 0.1 reshape.19.row_s
  33.8 1.7 %gather_rows.1 = bf16[256,8,96]{2,1,0:T(8,128)(2,1)} custom-call(s32[256]{0:T(256)S(1)} %reshape.19.row_s, bf16[64,8,96]{2,1,0:T(8,128)(2,1)S(1)} %reshape.20.from_ref.table_ref), custom_call_target="tpu_custom_call" | custom-call | tf_op jit(solution)/shard_map/gather_rows/pallas_call | solution.py:186
  35.6 6.0 %all-to-all-start.1 = ((bf16[256,8,96]{2,1,0:T(8,128)(2,1)}), bf16[256,8,96]{2,1,0:T(8,128)(2,1)S(1)}, u32[]{:S(2)}, u32[]{:S(2)}) async-start(bf16[256,8,96]{2,1,0:T(8,128)(2,1)} %gather_rows.1), calls=%async_computation.1 | async-start | bytes 1048576 | tf_op jit(solution)/shard_map/all_to_all | solution.py:255
  41.6 0.0 copy-done.2
  41.6 0.0 copy-done
  41.6 0.0 copy-done.1
  41.6 16.9 %mirror_pass.2 = f32[192,8,128]{2,1,0:T(8,128)} custom-call(s32[1024]{0:T(1024)S(1)} %copy-done.1, s32[1024]{0:T(1024)S(1)} %copy-done, s32[1024]{0:T(1024)S(1)} %copy-done.2, bf16[512,96,256]{2,1,0:T(8,128)(2,1)} %pair_tiles.1.pairs_ref, bf16[64,8,96]{2,1,0:T(8,128)(2,1)S(1)} %reshape.20.from_ref.table_ref), custom_call_target="tpu_custom_call" | custom-call | flops 150994944 | bytes 25165824 | tf_op jit(solution)/shard_map/mirror_pass/pallas_call | solution.py:145
  58.6 0.0 all-to-all-done.1.table_ref
  58.6 6.0 %all-to-all-start.2 = ((f32[192,8,128]{2,1,0:T(8,128)}), f32[192,8,128]{2,1,0:T(8,128)S(1)}, u32[]{:S(2)}, u32[]{:S(2)}) async-start(f32[192,8,128]{2,1,0:T(8,128)} %mirror_pass.2), calls=%async_computation.2 | async-start | bytes 1572864 | tf_op jit(solution)/shard_map/all_to_all | solution.py:257
  64.6 15.2 %direct_pass.2.own_ref = f32[64,8,96]{2,1,0:T(8,128)S(1)} custom-call(s32[1024]{0:T(1024)S(1)} %copy-done, s32[1024]{0:T(1024)S(1)} %copy-done.1, s32[1024]{0:T(1024)S(1)} %copy-done.2, bf16[512,96,256]{2,1,0:T(8,128)(2,1)} %pair_tiles.1.pairs_ref, bf16[256,8,96]{2,1,0:T(8,128)(2,1)S(1)} %all-to-all-done.1.table_ref), custom_call_target="tpu_custom_call" | custom-call | flops 150994944 | bytes 25165824 | tf_op jit(solution)/shard_map/direct_pass/pallas_call | solution.py:145
  79.7 4.4 %all-to-all-done.2.got_ref = f32[192,8,128]{2,1,0:T(8,128)S(1)} async-done(((f32[192,8,128]{2,1,0:T(8,128)}), f32[192,8,128]{2,1,0:T(8,128)S(1)}, u32[]{:S(2)}, u32[]{:S(2)}) %all-to-all-start.2) | async-done | bytes 786464 | tf_op jit(solution)/shard_map/all_to_all | solution.py:257
  84.1 3.1 %combine_rows.2 = (bf16[64,8,96]{2,1,0:T(8,128)(2,1)S(1)}, bf16[256,8,96]{2,1,0:T(8,128)(2,1)}) custom-call(s32[256]{0:T(256)S(1)} %reshape.19.row_s, f32[64,8,96]{2,1,0:T(8,128)S(1)} %direct_pass.2.own_ref, f32[192,8,128]{2,1,0:T(8,128)S(1)} %all-to-all-done.2.got_ref), custom_call_target="tpu_custom_call" | custom-call | tf_op jit(solution)/shard_map/combine_rows/pallas_call | solution.py:233
  87.2 4.6 %all-to-all-start.3 = ((bf16[256,8,96]{2,1,0:T(8,128)(2,1)}), bf16[256,8,96]{2,1,0:T(8,128)(2,1)S(1)}, u32[]{:S(2)}, u32[]{:S(2)}) async-start(bf16[256,8,96]{2,1,0:T(8,128)(2,1)} %get-tuple-element.9), calls=%async_computation.3 | async-start | bytes 1048576 | tf_op jit(solution)/shard_map/all_to_all | solution.py:255
  91.9 16.9 %mirror_pass.3 = f32[192,8,128]{2,1,0:T(8,128)} custom-call(s32[1024]{0:T(1024)S(1)} %copy-done.1, s32[1024]{0:T(1024)S(1)} %copy-done, s32[1024]{0:T(1024)S(1)} %copy-done.2, bf16[512,96,256]{2,1,0:T(8,128)(2,1)} %pair_tiles.1.pairs_ref, bf16[64,8,96]{2,1,0:T(8,128)(2,1)S(1)} %get-tuple-element.8.table_ref), custom_call_target="tpu_custom_call" | custom-call | flops 150994944 | bytes 25165824 | tf_op jit(solution)/shard_map/mirror_pass/pallas_call | solution.py:145
  108.8 0.0 all-to-all-done.3.table_ref
  108.8 6.0 %all-to-all-start.4 = ((f32[192,8,128]{2,1,0:T(8,128)}), f32[192,8,128]{2,1,0:T(8,128)S(1)}, u32[]{:S(2)}, u32[]{:S(2)}) async-start(f32[192,8,128]{2,1,0:T(8,128)} %mirror_pass.3), calls=%async_computation.4 | async-start | bytes 1572864 | tf_op jit(solution)/shard_map/all_to_all | solution.py:257
  114.8 0.8 reshape.21
  115.6 15.2 %direct_pass.3.own_ref = f32[64,8,96]{2,1,0:T(8,128)S(1)} custom-call(s32[1024]{0:T(1024)S(1)} %copy-done, s32[1024]{0:T(1024)S(1)} %copy-done.1, s32[1024]{0:T(1024)S(1)} %copy-done.2, bf16[512,96,256]{2,1,0:T(8,128)(2,1)} %pair_tiles.1.pairs_ref, bf16[256,8,96]{2,1,0:T(8,128)(2,1)S(1)} %all-to-all-done.3.table_ref), custom_call_target="tpu_custom_call" | custom-call | flops 150994944 | bytes 25165824 | tf_op jit(solution)/shard_map/direct_pass/pallas_call | solution.py:145
  130.8 3.6 %all-to-all-done.4.got_ref = f32[192,8,128]{2,1,0:T(8,128)S(1)} async-done(((f32[192,8,128]{2,1,0:T(8,128)}), f32[192,8,128]{2,1,0:T(8,128)S(1)}, u32[]{:S(2)}, u32[]{:S(2)}) %all-to-all-start.4) | async-done | bytes 786464 | tf_op jit(solution)/shard_map/all_to_all | solution.py:257
  134.4 2.0 %combine_rows.3 = bf16[64,8,96]{2,1,0:T(8,128)(2,1)S(1)} custom-call(s32[256]{0:T(256)S(1)} %reshape.19.row_s, f32[64,8,96]{2,1,0:T(8,128)S(1)} %direct_pass.3.own_ref, f32[192,8,128]{2,1,0:T(8,128)S(1)} %all-to-all-done.4.got_ref), custom_call_target="tpu_custom_call" | custom-call | tf_op jit(solution)/shard_map/combine_rows/pallas_call | solution.py:233
  136.4 0.8 reshape.22
Async XLA Ops:
  0.6 41.0 %copy-start.2 = (s32[1024]{0:T(1024)S(1)}, s32[1024]{0:T(1024)}, u32[]{:S(2)}) copy-start(s32[1024]{0:T(1024)} %flag_s.7) | copy-start | bytes 12292
  0.6 41.0 %copy-start = (s32[1024]{0:T(1024)S(1)}, s32[1024]{0:T(1024)}, u32[]{:S(2)}) copy-start(s32[1024]{0:T(1024)} %put_s.7) | copy-start | bytes 12292
  0.7 41.0 %copy-start.1 = (s32[1024]{0:T(1024)S(1)}, s32[1024]{0:T(1024)}, u32[]{:S(2)}) copy-start(s32[1024]{0:T(1024)} %pick_s.7) | copy-start | bytes 12292
  0.7 33.1 %all-to-all-start = ((s32[16,1,16]{2,1,0:T(1,128)}), s32[16,1,16]{2,1,0:T(1,128)S(1)}, u32[]{:S(2)}, u32[]{:S(2)}) async-start(s32[16,1,16]{2,1,0:T(1,128)} %bitcast.5), calls=%async_computation | async-start | bytes 16384 | tf_op jit(solution)/shard_map/all_to_all | solution.py:251
  35.6 23.0 %all-to-all-start.1 = ((bf16[256,8,96]{2,1,0:T(8,128)(2,1)}), bf16[256,8,96]{2,1,0:T(8,128)(2,1)S(1)}, u32[]{:S(2)}, u32[]{:S(2)}) async-start(bf16[256,8,96]{2,1,0:T(8,128)(2,1)} %gather_rows.1), calls=%async_computation.1 | async-start | bytes 1048576 | tf_op jit(solution)/shard_map/all_to_all | solution.py:255
  58.6 25.6 %all-to-all-start.2 = ((f32[192,8,128]{2,1,0:T(8,128)}), f32[192,8,128]{2,1,0:T(8,128)S(1)}, u32[]{:S(2)}, u32[]{:S(2)}) async-start(f32[192,8,128]{2,1,0:T(8,128)} %mirror_pass.2), calls=%async_computation.2 | async-start | bytes 1572864 | tf_op jit(solution)/shard_map/all_to_all | solution.py:257
  87.2 21.6 %all-to-all-start.3 = ((bf16[256,8,96]{2,1,0:T(8,128)(2,1)}), bf16[256,8,96]{2,1,0:T(8,128)(2,1)S(1)}, u32[]{:S(2)}, u32[]{:S(2)}) async-start(bf16[256,8,96]{2,1,0:T(8,128)(2,1)} %get-tuple-element.9), calls=%async_computation.3 | async-start | bytes 1048576 | tf_op jit(solution)/shard_map/all_to_all | solution.py:255
  108.8 25.6 %all-to-all-start.4 = ((f32[192,8,128]{2,1,0:T(8,128)}), f32[192,8,128]{2,1,0:T(8,128)S(1)}, u32[]{:S(2)}, u32[]{:S(2)}) async-start(f32[192,8,128]{2,1,0:T(8,128)} %mirror_pass.3), calls=%async_computation.4 | async-start | bytes 1572864 | tf_op jit(solution)/shard_map/all_to_all | solution.py:257

commit v6 on v5

--- a/solution.py
+++ b/solution.py
@@ -16,44 +16,26 @@
 PITCH = BLOCK + 8
 
 
-def pair_kernel(tiles_ref, out_ref, turned_ref):
-    unknowns = tiles_ref.shape[0]
-    half = BLOCK // 2
-    blank = jnp.zeros((LANES - unknowns, BLOCK), tiles_ref.dtype)
-
-    def turn(g, carry):
-        for u in range(8):
-            i = g * 8 + u
-            turned = jnp.concatenate([tiles_ref[i], blank], axis=0).T
-            turned_ref[pl.ds(pl.multiple_of(i * PITCH, 8), BLOCK), :] = turned.astype(jnp.float32)
-        return carry
-
-    lax.fori_loop(0, unknowns // 8, turn, 0)
+def turn_row(i, tiles_ref, turned_ref):
+    blank = jnp.zeros((LANES - tiles_ref.shape[1], BLOCK), tiles_ref.dtype)
+    turned = jnp.concatenate([tiles_ref[i], blank], axis=0).T
+    turned_ref[pl.ds(pl.multiple_of(i * PITCH, 8), BLOCK), :] = turned.astype(jnp.float32)
+
+
+def place_pairs(turned_ref, out_refs):
+    half, unknowns = out_refs[0].shape[0], out_refs[0].shape[1]
 
     def place(g, carry):
         for u in range(4):
             p = g * 4 + u
             low = turned_ref[pl.ds(p, unknowns, stride=PITCH), :]
             high = turned_ref[pl.ds(p + half, unknowns, stride=PITCH), :]
-            out_ref[p] = jnp.concatenate([low, high], axis=1).astype(out_ref.dtype)
+            pair = jnp.concatenate([low, high], axis=1).astype(out_refs[0].dtype)
+            for ref in out_refs:
+                ref[p] = pair
         return carry
 
     lax.fori_loop(0, half // 4, place, 0)
-
-
-def pair_tiles(tiles):
-    count, unknowns = tiles.shape[0], tiles.shape[1]
-    return pl.pallas_call(
-        pair_kernel,
-        out_shape=jax.ShapeDtypeStruct((count // 2, unknowns, 2 * LANES), tiles.dtype),
-        grid=(count // BLOCK,),
-        in_specs=[pl.BlockSpec((unknowns, unknowns, BLOCK), lambda s: (0, 0, s))],
-        out_specs=pl.BlockSpec((BLOCK // 2, unknowns, 2 * LANES), lambda s: (s, 0, 0)),
-        scratch_shapes=[pltpu.VMEM((unknowns * PITCH, LANES), jnp.float32)],
-        compiler_params=pltpu.CompilerParams(vmem_limit_bytes=48 * 2**20),
-        cost_estimate=pl.CostEstimate(flops=0, bytes_accessed=44 * 2**20, transcendentals=0),
-        name="pair_tiles",
-    )(jnp.transpose(tiles, (1, 2, 0)))
 
 
 def pack_slots(banks, out_ref, unknowns, capacity):
@@ -76,25 +58,21 @@
     lax.fori_loop(0, out_ref.shape[0] // kept, peer, 0)
 
 
-def pass_kernel(mirrored, capacity, pick_s, put_s, flag_s, pairs_ref, table_ref, out_ref, near_ref, *banks):
-    step = pl.program_id(0)
-    unknowns = pairs_ref.shape[1]
-    half = BLOCK // 2
-
-    @pl.when(step == 0)
-    def _():
-        for bank in banks:
-            bank[...] = jnp.zeros_like(bank)
-        values = table_ref[...].astype(jnp.float32)
-        if mirrored:
-            blank = jnp.zeros_like(values)
-            near_ref[0] = jnp.concatenate([values, blank], axis=2)
-            near_ref[1] = jnp.concatenate([blank, values], axis=2)
-        else:
-            blank = jnp.zeros(values.shape[:2] + (LANES - unknowns,), jnp.float32)
-            near_ref[0] = jnp.concatenate([values, blank], axis=2)
-
-    base = step * BLOCK
+def prepare(mirrored, table_ref, near_ref, banks):
+    for bank in banks:
+        bank[...] = jnp.zeros_like(bank)
+    values = table_ref[...].astype(jnp.float32)
+    if mirrored:
+        blank = jnp.zeros_like(values)
+        near_ref[0] = jnp.concatenate([values, blank], axis=2)
+        near_ref[1] = jnp.concatenate([blank, values], axis=2)
+    else:
+        blank = jnp.zeros(values.shape[:2] + (LANES - values.shape[2],), jnp.float32)
+        near_ref[0] = jnp.concatenate([values, blank], axis=2)
+
+
+def apply_four(mirrored, base, p, pick_s, put_s, flag_s, pairs_ref, near_ref, banks):
+    half, unknowns = pairs_ref.shape[0], pairs_ref.shape[1]
     empty = jnp.zeros((NRHS, LANES), jnp.float32)
 
     def operand(k, place):
@@ -103,24 +81,37 @@
         x = near_ref[0, pick_s[k]]
         return jnp.concatenate([empty, x] if place % 2 else [x, empty], axis=1)
 
+    k = base + p
+    members = (k, k + half, k + 1, k + 1 + half)
+    rows = jnp.concatenate([operand(m, n) for n, m in enumerate(members)], axis=0)
+    stacked = pairs_ref[pl.ds(p, 2)].reshape(2 * unknowns, 2 * LANES)
+    dims = (((1,), (0 if mirrored else 1,)), ((), ()))
+    product = lax.dot_general(
+        rows.astype(jnp.bfloat16), stacked, dims, preferred_element_type=jnp.float32
+    )
+    for n, m in enumerate(members):
+        part = product[n * NRHS:(n + 1) * NRHS]
+        if mirrored:
+            part = part[:, (n % 2) * LANES:(n % 2 + 1) * LANES]
+        else:
+            part = part[:, :banks[n].shape[2]]
+        banks[n][put_s[m]] += part
+
+
+def pass_kernel(mirrored, capacity, pick_s, put_s, flag_s, pairs_ref, table_ref, out_ref, near_ref, *banks):
+    step = pl.program_id(0)
+    unknowns = pairs_ref.shape[1]
+
+    @pl.when(step == 0)
+    def _():
+        prepare(mirrored, table_ref, near_ref, banks)
+
     def group(g, carry):
         start = pl.multiple_of(g * (UNROLL // 2), UNROLL // 2)
         for u in range(0, UNROLL // 2, 2):
-            k = base + start + u
-            members = (k, k + half, k + 1, k + 1 + half)
-            rows = jnp.concatenate([operand(m, n) for n, m in enumerate(members)], axis=0)
-            stacked = pairs_ref[pl.ds(start + u, 2)].reshape(2 * unknowns, 2 * LANES)
-            dims = (((1,), (0 if mirrored else 1,)), ((), ()))
-            product = lax.dot_general(
-                rows.astype(jnp.bfloat16), stacked, dims, preferred_element_type=jnp.float32
+            apply_four(
+                mirrored, step * BLOCK, start + u, pick_s, put_s, flag_s, pairs_ref, near_ref, banks
             )
-            for n, m in enumerate(members):
-                part = product[n * NRHS:(n + 1) * NRHS]
-                if mirrored:
-                    part = part[:, (n % 2) * LANES:(n % 2 + 1) * LANES]
-                else:
-                    part = part[:, :banks[n].shape[2]]
-                banks[n][put_s[m]] += part
         return carry
 
     lax.fori_loop(0, BLOCK // UNROLL, group, 0)
@@ -132,6 +123,96 @@
         else:
             low, high = banks[0][...] + banks[1][...], banks[2][...] + banks[3][...]
             out_ref[...] = low[:, :, :unknowns] + high[:, :, unknowns:]
+
+
+def first_kernel(
+    capacity, pick_s, put_s, flag_s, tiles_ref, table_ref, pairs_ref, out_ref,
+    turned_ref, held_ref, near_ref, *banks
+):
+    step = pl.program_id(0)
+    last = pl.num_programs(0) - 1
+    unknowns = tiles_ref.shape[0]
+    rounds = 8
+    pairs = BLOCK // 2 // rounds
+
+    @pl.when(step == 0)
+    def _():
+        prepare(True, table_ref, near_ref, banks)
+
+    def work(turning, applying):
+        def group(g, carry):
+            for u in range(0, pairs, 2):
+                if turning:
+                    count = 2 * unknowns // rounds // pairs
+                    for t in range(count):
+                        i = g * (unknowns // rounds) + u // 2 * count + t
+                        turn_row(i, tiles_ref, turned_ref)
+                if applying:
+                    apply_four(
+                        True, (step - 1) * BLOCK, g * pairs + u,
+                        pick_s, put_s, flag_s, held_ref, near_ref, banks
+                    )
+            return carry
+
+        lax.fori_loop(0, rounds, group, 0)
+
+    @pl.when(step == 0)
+    def _():
+        work(True, False)
+
+    @pl.when(jnp.logical_and(step > 0, step < last))
+    def _():
+        work(True, True)
+
+    @pl.when(step < last)
+    def _():
+        place_pairs(turned_ref, (pairs_ref, held_ref))
+
+    @pl.when(step == last)
+    def _():
+        work(False, True)
+        pack_slots(banks, out_ref, unknowns, capacity)
+
+
+def first_pass(pick, put, flag, tiles, table, rows, capacity):
+    count, unknowns = tiles.shape[0], tiles.shape[1]
+    blocks = count // BLOCK
+    out = (rows * unknowns // LANES, NRHS, LANES)
+    pair_shape = (BLOCK // 2, unknowns, 2 * LANES)
+    return pl.pallas_call(
+        functools.partial(first_kernel, capacity),
+        out_shape=[
+            jax.ShapeDtypeStruct((count // 2,) + pair_shape[1:], tiles.dtype),
+            jax.ShapeDtypeStruct(out, jnp.float32),
+        ],
+        grid_spec=pltpu.PrefetchScalarGridSpec(
+            num_scalar_prefetch=3,
+            grid=(blocks + 1,),
+            in_specs=[
+                pl.BlockSpec(
+                    (unknowns, unknowns, BLOCK), lambda s, *_: (0, 0, jnp.minimum(s, blocks - 1))
+                ),
+                pl.BlockSpec(table.shape, lambda s, *_: (0, 0, 0)),
+            ],
+            out_specs=[
+                pl.BlockSpec(pair_shape, lambda s, *_: (jnp.minimum(s, blocks - 1), 0, 0)),
+                pl.BlockSpec(out, lambda s, *_: (0, 0, 0)),
+            ],
+            scratch_shapes=[
+                pltpu.VMEM((unknowns * PITCH, LANES), jnp.float32),
+                pltpu.VMEM(pair_shape, tiles.dtype),
+                pltpu.VMEM((2, table.shape[0], NRHS, 2 * unknowns), jnp.float32),
+            ]
+            + [pltpu.VMEM((rows, NRHS, LANES), jnp.float32)] * BANKS,
+        ),
+        compiler_params=pltpu.CompilerParams(vmem_limit_bytes=52 * 2**20),
+        cost_estimate=pl.CostEstimate(
+            flops=2 * count * NRHS * unknowns * unknowns,
+            bytes_accessed=44 * 2**20,
+            transcendentals=0,
+        ),
+        name="pair_and_mirror",
+    )(pick, put, flag, jnp.transpose(tiles, (1, 2, 0)), table)
 
 
 def tile_pass(mirrored, pick, put, flag, pairs, table, rows, capacity):
@@ -248,19 +329,20 @@
     capacity = want_list.shape[2]
     slots = peers * capacity
     wanted = want_list[0]
-    asked = lax.all_to_all(wanted, "row", 0, 0, tiled=True)
-    asked, pairs = lax.optimization_barrier((asked, pair_tiles(tiles)))
-    asked = asked.reshape(-1)
-    def operate(current, sent, again):
+    start = forces.reshape(fibres, NRHS, unknowns)
+    asked = lax.all_to_all(wanted, "row", 0, 0, tiled=True).reshape(-1)
+    first_sent, start = lax.optimization_barrier((gather(asked, start), start))
+    pairs, mirrored = first_pass(tile_local, tile_slot, tile_flag, tiles, start, slots, capacity)
+
+    def finish(mirrored, sent, again):
+        got = lax.all_to_all(mirrored, "row", 0, 0, tiled=True)
         far = lax.all_to_all(sent, "row", 0, 0, tiled=True)
-        slot_part = tile_pass(True, tile_local, tile_slot, tile_flag, pairs, current, slots, capacity)
-        got = lax.all_to_all(slot_part, "row", 0, 0, tiled=True)
-        own_part = tile_pass(False, tile_slot, tile_local, tile_flag, pairs, far, fibres, capacity)
-        return combine(asked, own_part, got, capacity, again)
-
-    start = forces.reshape(fibres, NRHS, unknowns)
-    one, sent = operate(start, gather(asked, start), True)
-    (two,) = operate(one, sent, False)
+        own = tile_pass(False, tile_slot, tile_local, tile_flag, pairs, far, fibres, capacity)
+        return combine(asked, own, got, capacity, again)
+
+    one, sent = finish(mirrored, first_sent, True)
+    mirrored = tile_pass(True, tile_local, tile_slot, tile_flag, pairs, one, slots, capacity)
+    (two,) = finish(mirrored, sent, False)
     return (one.reshape(fibres, width), two.reshape(fibres, width))
 
 

time: 139 us -> 133 us (0.957)
  Pallas kernels: 96.3 us -> 85.4 us
  local copies, waits for them, and re-layouts: 2.71 us -> 7.33 us
  waiting for transfers between devices: 7.98 us -> 9.49 us
    pallas_call x4 -> x3, Pallas kernels: 64.2 us -> 47.3 us  [tile_pass(): pl.pallas_call(functools.partial(pass_kernel, mirrored, capacity), out_sh...]
    pallas_call x1, Pallas kernels: 25.3 us -> 31.3 us  [first_pass(): pl.pallas_call(functools.partial(first_kernel, capacity), out_shape=[jax....]
    unnamed x6 -> x18, local copies, waits for them, and re-layouts: 0.01 us -> 4.12 us
    all_to_all x5, waiting for transfers between devices: 7.98 us -> 9.49 us  [the longest x2 5.92 us: finish(): got = lax.all_to_all(mirrored, 'row', 0, 0, tiled=True)]
  transfers between devices with their start and end apart: 5 -> 5, of which waited for: 2 -> 3; matrix products, arithmetic and copies ran while one was open for 1% -> 1% of each run, Pallas kernels for 65% -> 59%
where the time goes in v6:
time: 133 us; the launch traced here: 132 us
  Pallas kernels  85.4 us (64%)
  starting transfers between devices  28.5 us (21%)
  waiting for transfers between devices  9.49 us (7%)
  local copies, waits for them, and re-layouts  7.33 us (6%)
    pallas_call x3, Pallas kernels, tile_pass(): pl.pallas_call(functools.partial(pass_kernel, mirrored, capacity), out_sh...  47.3 us
    pallas_call x1, Pallas kernels, first_pass(): pl.pallas_call(functools.partial(first_kernel, capacity), out_shape=[jax....  31.3 us
    all_to_all x2, starting transfers between devices, finish(): got = lax.all_to_all(mirrored, 'row', 0, 0, tiled=True)  12.1 us
    all_to_all x2, starting transfers between devices, finish(): far = lax.all_to_all(sent, 'row', 0, 0, tiled=True)  9.82 us
    all_to_all x1, starting transfers between devices, per_device(): asked = lax.all_to_all(wanted, 'row', 0, 0, tiled=True).reshape(-1)  6.62 us
    all_to_all x2, waiting for transfers between devices, finish(): got = lax.all_to_all(mirrored, 'row', 0, 0, tiled=True)  5.92 us
    pallas_call x2, Pallas kernels, combine(): pl.pallas_call(functools.partial(combine_kernel, capacity), out_shape=out...  5.09 us
    unnamed x18, local copies, waits for them, and re-layouts  4.12 us
  transfers between devices with their start and end apart: 5, of which 3 were waited for; matrix products, arithmetic and copies ran while one was open for 1% of the time, Pallas kernels for 59%

profile of v6, /device:TPU:9, one launch (start us, length us, event | category | flops | bytes accessed | tf_op | source)
XLA Modules:
  0.0 132.2 jit_solution(3967201490807819637)
XLA Ops:
  0.6 6.6 %all-to-all-start = ((s32[16,1,16]{2,1,0:T(1,128)}), s32[16,1,16]{2,1,0:T(1,128)S(1)}, u32[]{:S(2)}, u32[]{:S(2)}) async-start(s32[16,1,16]{2,1,0:T(1,128)} %bitcast.3), calls=%async_computation | async-start | bytes 16384 | tf_op jit(solution)/shard_map/all_to_all | solution.py:333
  7.3 1.0 reshape.21.from_ref.table_ref
  8.3 3.6 %all-to-all-done = s32[16,1,16]{2,1,0:T(1,128)S(1)} async-done(((s32[16,1,16]{2,1,0:T(1,128)}), s32[16,1,16]{2,1,0:T(1,128)S(1)}, u32[]{:S(2)}, u32[]{:S(2)}) %all-to-all-start) | async-done | bytes 1056 | tf_op jit(solution)/shard_map/all_to_all | solution.py:333
  11.9 0.5 broadcast.3
  12.4 0.7 reduce.3
  13.1 0.1 reshape.20.row_s
  13.1 0.0 copy-start.2
  13.1 0.0 copy-start.5
  13.1 0.0 copy-start.8
  13.2 1.7 %gather_rows.1 = bf16[256,8,96]{2,1,0:T(8,128)(2,1)} custom-call(s32[256]{0:T(256)S(1)} %reshape.20.row_s, bf16[64,8,96]{2,1,0:T(8,128)(2,1)S(1)} %reshape.21.from_ref.table_ref), custom_call_target="tpu_custom_call" | custom-call | tf_op jit(solution)/shard_map/gather_rows/pallas_call | solution.py:267
  14.9 5.2 %all-to-all-start.1 = ((bf16[256,8,96]{2,1,0:T(8,128)(2,1)}), bf16[256,8,96]{2,1,0:T(8,128)(2,1)S(1)}, u32[]{:S(2)}, u32[]{:S(2)}) async-start(bf16[256,8,96]{2,1,0:T(8,128)(2,1)} %gather_rows.1), calls=%async_computation.1 | async-start | bytes 1048576 | tf_op jit(solution)/shard_map/all_to_all | solution.py:339
  20.1 0.0 copy-start
  20.1 0.7 copy-done
  20.8 0.0 copy-start.3
  20.8 0.7 copy-done.3
  21.4 0.0 copy-start.6
  21.4 0.7 copy-done.6
  22.1 31.3 %pair_and_mirror.1 = (bf16[512,96,256]{2,1,0:T(8,128)(2,1)}, f32[192,8,128]{2,1,0:T(8,128)}) custom-call(s32[1024]{0:T(1024)S(1)} %copy-done.3, s32[1024]{0:T(1024)S(1)} %copy-done, s32[1024]{0:T(1024)S(1)} %copy-done.6, bf16[96,96,1024]{2,1,0:T(8,128)(2,1)} %bitcast.2, bf16[64,8,96]{2,1,0:T(8,128)(2,1)S(1)} %reshape.21.from_ref.table_ref), custom_call_target="tpu_custom_call" | custom-call | flops 150994944 | bytes 46137344 | tf_op jit(solution)/shard_map/pair_and_mirror/pallas_call | solution.py:182
  53.4 0.0 all-to-all-done.1.table_ref
  53.4 6.1 %all-to-all-start.2 = ((f32[192,8,128]{2,1,0:T(8,128)}), f32[192,8,128]{2,1,0:T(8,128)S(1)}, u32[]{:S(2)}, u32[]{:S(2)}) async-start(f32[192,8,128]{2,1,0:T(8,128)} %get-tuple-element.11), calls=%async_computation.2 | async-start | bytes 1572864 | tf_op jit(solution)/shard_map/all_to_all | solution.py:338
  59.5 0.0 copy-start.1
  59.5 0.7 copy-done.1
  60.2 0.0 copy-start.4
  60.2 0.7 copy-done.4
  60.9 0.0 copy-start.7
  60.9 0.7 copy-done.7
  61.6 15.2 %direct_pass.2.own_ref = f32[64,8,96]{2,1,0:T(8,128)S(1)} custom-call(s32[1024]{0:T(1024)S(1)} %copy-done.1, s32[1024]{0:T(1024)S(1)} %copy-done.4, s32[1024]{0:T(1024)S(1)} %copy-done.7, bf16[512,96,256]{2,1,0:T(8,128)(2,1)} %get-tuple-element.9.pairs_ref, bf16[256,8,96]{2,1,0:T(8,128)(2,1)S(1)} %all-to-all-done.1.table_ref), custom_call_target="tpu_custom_call" | custom-call | flops 150994944 | bytes 25165824 | tf_op jit(solution)/shard_map/direct_pass/pallas_call | solution.py:226
  76.8 2.3 %all-to-all-done.2.got_ref = f32[192,8,128]{2,1,0:T(8,128)S(1)} async-done(((f32[192,8,128]{2,1,0:T(8,128)}), f32[192,8,128]{2,1,0:T(8,128)S(1)}, u32[]{:S(2)}, u32[]{:S(2)}) %all-to-all-start.2) | async-done | bytes 786464 | tf_op jit(solution)/shard_map/all_to_all | solution.py:338
  79.1 3.1 %combine_rows.2 = (bf16[64,8,96]{2,1,0:T(8,128)(2,1)S(1)}, bf16[256,8,96]{2,1,0:T(8,128)(2,1)}) custom-call(s32[256]{0:T(256)S(1)} %reshape.20.row_s, f32[64,8,96]{2,1,0:T(8,128)S(1)} %direct_pass.2.own_ref, f32[192,8,128]{2,1,0:T(8,128)S(1)} %all-to-all-done.2.got_ref), custom_call_target="tpu_custom_call" | custom-call | tf_op jit(solution)/shard_map/combine_rows/pallas_call | solution.py:314
  82.2 4.6 %all-to-all-start.3 = ((bf16[256,8,96]{2,1,0:T(8,128)(2,1)}), bf16[256,8,96]{2,1,0:T(8,128)(2,1)S(1)}, u32[]{:S(2)}, u32[]{:S(2)}) async-start(bf16[256,8,96]{2,1,0:T(8,128)(2,1)} %get-tuple-element.13), calls=%async_computation.3 | async-start | bytes 1048576 | tf_op jit(solution)/shard_map/all_to_all | solution.py:339
  86.8 0.0 copy-done.2
  86.8 0.0 copy-done.5
  86.9 0.0 copy-done.8
  86.9 17.0 %mirror_pass.1 = f32[192,8,128]{2,1,0:T(8,128)} custom-call(s32[1024]{0:T(1024)S(1)} %copy-done.5, s32[1024]{0:T(1024)S(1)} %copy-done.2, s32[1024]{0:T(1024)S(1)} %copy-done.8, bf16[512,96,256]{2,1,0:T(8,128)(2,1)} %get-tuple-element.9.pairs_ref, bf16[64,8,96]{2,1,0:T(8,128)(2,1)S(1)} %get-tuple-element.12.table_ref), custom_call_target="tpu_custom_call" | custom-call | flops 150994944 | bytes 25165824 | tf_op jit(solution)/shard_map/mirror_pass/pallas_call | solution.py:226
  103.8 0.0 all-to-all-done.3.table_ref
  103.8 6.0 %all-to-all-start.4 = ((f32[192,8,128]{2,1,0:T(8,128)}), f32[192,8,128]{2,1,0:T(8,128)S(1)}, u32[]{:S(2)}, u32[]{:S(2)}) async-start(f32[192,8,128]{2,1,0:T(8,128)} %mirror_pass.1), calls=%async_computation.4 | async-start | bytes 1572864 | tf_op jit(solution)/shard_map/all_to_all | solution.py:338
  109.8 0.8 reshape.22
  110.6 15.2 %direct_pass.3.own_ref = f32[64,8,96]{2,1,0:T(8,128)S(1)} custom-call(s32[1024]{0:T(1024)S(1)} %copy-done.2, s32[1024]{0:T(1024)S(1)} %copy-done.5, s32[1024]{0:T(1024)S(1)} %copy-done.8, bf16[512,96,256]{2,1,0:T(8,128)(2,1)} %get-tuple-element.9.pairs_ref, bf16[256,8,96]{2,1,0:T(8,128)(2,1)S(1)} %all-to-all-done.3.table_ref), custom_call_target="tpu_custom_call" | custom-call | flops 150994944 | bytes 25165824 | tf_op jit(solution)/shard_map/direct_pass/pallas_call | solution.py:226
  125.8 3.6 %all-to-all-done.4.got_ref = f32[192,8,128]{2,1,0:T(8,128)S(1)} async-done(((f32[192,8,128]{2,1,0:T(8,128)}), f32[192,8,128]{2,1,0:T(8,128)S(1)}, u32[]{:S(2)}, u32[]{:S(2)}) %all-to-all-start.4) | async-done | bytes 786464 | tf_op jit(solution)/shard_map/all_to_all | solution.py:338
  129.4 2.0 %combine_rows.3 = bf16[64,8,96]{2,1,0:T(8,128)(2,1)S(1)} custom-call(s32[256]{0:T(256)S(1)} %reshape.20.row_s, f32[64,8,96]{2,1,0:T(8,128)S(1)} %direct_pass.3.own_ref, f32[192,8,128]{2,1,0:T(8,128)S(1)} %all-to-all-done.4.got_ref), custom_call_target="tpu_custom_call" | custom-call | tf_op jit(solution)/shard_map/combine_rows/pallas_call | solution.py:314
  131.4 0.8 reshape.23
Async XLA Ops:
  0.6 11.2 %all-to-all-start = ((s32[16,1,16]{2,1,0:T(1,128)}), s32[16,1,16]{2,1,0:T(1,128)S(1)}, u32[]{:S(2)}, u32[]{:S(2)}) async-start(s32[16,1,16]{2,1,0:T(1,128)} %bitcast.3), calls=%async_computation | async-start | bytes 16384 | tf_op jit(solution)/shard_map/all_to_all | solution.py:333
  13.1 73.7 %copy-start.2 = (s32[1024]{0:T(1024)S(1)}, s32[1024]{0:T(1024)}, u32[]{:S(2)}) copy-start(s32[1024]{0:T(1024)} %put_s.7) | copy-start | bytes 12292
  13.1 73.7 %copy-start.5 = (s32[1024]{0:T(1024)S(1)}, s32[1024]{0:T(1024)}, u32[]{:S(2)}) copy-start(s32[1024]{0:T(1024)} %pick_s.7) | copy-start | bytes 12292
  13.1 73.7 %copy-start.8 = (s32[1024]{0:T(1024)S(1)}, s32[1024]{0:T(1024)}, u32[]{:S(2)}) copy-start(s32[1024]{0:T(1024)} %flag_s.7) | copy-start | bytes 12292
  14.9 38.6 %all-to-all-start.1 = ((bf16[256,8,96]{2,1,0:T(8,128)(2,1)}), bf16[256,8,96]{2,1,0:T(8,128)(2,1)S(1)}, u32[]{:S(2)}, u32[]{:S(2)}) async-start(bf16[256,8,96]{2,1,0:T(8,128)(2,1)} %gather_rows.1), calls=%async_computation.1 | async-start | bytes 1048576 | tf_op jit(solution)/shard_map/all_to_all | solution.py:339
  20.1 0.7 copy-start
  20.8 0.7 copy-start.3
  21.4 0.7 copy-start.6
  53.4 25.6 %all-to-all-start.2 = ((f32[192,8,128]{2,1,0:T(8,128)}), f32[192,8,128]{2,1,0:T(8,128)S(1)}, u32[]{:S(2)}, u32[]{:S(2)}) async-start(f32[192,8,128]{2,1,0:T(8,128)} %get-tuple-element.11), calls=%async_computation.2 | async-start | bytes 1572864 | tf_op jit(solution)/shard_map/all_to_all | solution.py:338
  59.5 0.7 copy-start.1
  60.2 0.7 copy-start.4
  60.9 0.7 copy-start.7
  82.2 21.6 %all-to-all-start.3 = ((bf16[256,8,96]{2,1,0:T(8,128)(2,1)}), bf16[256,8,96]{2,1,0:T(8,128)(2,1)S(1)}, u32[]{:S(2)}, u32[]{:S(2)}) async-start(bf16[256,8,96]{2,1,0:T(8,128)(2,1)} %get-tuple-element.13), calls=%async_computation.3 | async-start | bytes 1048576 | tf_op jit(solution)/shard_map/all_to_all | solution.py:339
  103.8 25.6 %all-to-all-start.4 = ((f32[192,8,128]{2,1,0:T(8,128)}), f32[192,8,128]{2,1,0:T(8,128)S(1)}, u32[]{:S(2)}, u32[]{:S(2)}) async-start(f32[192,8,128]{2,1,0:T(8,128)} %mirror_pass.1), calls=%async_computation.4 | async-start | bytes 1572864 | tf_op jit(solution)/shard_map/all_to_all | solution.py:338

commit v7 on v6

--- a/solution.py
+++ b/solution.py
@@ -9,7 +9,7 @@
 
 NRHS = 8
 BANKS = 4
-UNROLL = 64
+UNROLL = 128
 LANES = 128
 ROWS = 16
 BLOCK = 128
@@ -26,8 +26,8 @@
     half, unknowns = out_refs[0].shape[0], out_refs[0].shape[1]
 
     def place(g, carry):
-        for u in range(4):
-            p = g * 4 + u
+        for u in range(16):
+            p = g * 16 + u
             low = turned_ref[pl.ds(p, unknowns, stride=PITCH), :]
             high = turned_ref[pl.ds(p + half, unknowns, stride=PITCH), :]
             pair = jnp.concatenate([low, high], axis=1).astype(out_refs[0].dtype)
@@ -35,7 +35,7 @@
                 ref[p] = pair
         return carry
 
-    lax.fori_loop(0, half // 4, place, 0)
+    lax.fori_loop(0, half // 16, place, 0)
 
 
 def pack_slots(banks, out_ref, unknowns, capacity):
@@ -55,7 +55,7 @@
         )
         return carry
 
-    lax.fori_loop(0, out_ref.shape[0] // kept, peer, 0)
+    lax.fori_loop(0, out_ref.shape[0] // kept, peer, 0, unroll=4)
 
 
 def prepare(mirrored, table_ref, near_ref, banks):
@@ -71,14 +71,15 @@
         near_ref[0] = jnp.concatenate([values, blank], axis=2)
 
 
-def apply_four(mirrored, base, p, pick_s, put_s, flag_s, pairs_ref, near_ref, banks):
+def apply_four(mirrored, base, p, index_s, pairs_ref, near_ref, banks):
     half, unknowns = pairs_ref.shape[0], pairs_ref.shape[1]
     empty = jnp.zeros((NRHS, LANES), jnp.float32)
+    count = index_s.shape[0] // 3
 
     def operand(k, place):
         if mirrored:
-            return near_ref[place // 2, pick_s[k]] * flag_s[k].astype(jnp.float32)
-        x = near_ref[0, pick_s[k]]
+            return near_ref[place // 2, index_s[k]] * index_s[2 * count + k].astype(jnp.float32)
+        x = near_ref[0, index_s[count + k]]
         return jnp.concatenate([empty, x] if place % 2 else [x, empty], axis=1)
 
     k = base + p
@@ -95,10 +96,10 @@
             part = part[:, (n % 2) * LANES:(n % 2 + 1) * LANES]
         else:
             part = part[:, :banks[n].shape[2]]
-        banks[n][put_s[m]] += part
-
-
-def pass_kernel(mirrored, capacity, pick_s, put_s, flag_s, pairs_ref, table_ref, out_ref, near_ref, *banks):
+        banks[n][index_s[(count if mirrored else 0) + m]] += part
+
+
+def pass_kernel(mirrored, capacity, index_s, pairs_ref, table_ref, out_ref, near_ref, *banks):
     step = pl.program_id(0)
     unknowns = pairs_ref.shape[1]
 
@@ -110,7 +111,7 @@
         start = pl.multiple_of(g * (UNROLL // 2), UNROLL // 2)
         for u in range(0, UNROLL // 2, 2):
             apply_four(
-                mirrored, step * BLOCK, start + u, pick_s, put_s, flag_s, pairs_ref, near_ref, banks
+                mirrored, step * BLOCK, start + u, index_s, pairs_ref, near_ref, banks
             )
         return carry
 
@@ -126,13 +127,13 @@
 
 
 def first_kernel(
-    capacity, pick_s, put_s, flag_s, tiles_ref, table_ref, pairs_ref, out_ref,
+    capacity, index_s, tiles_ref, table_ref, pairs_ref, out_ref,
     turned_ref, held_ref, near_ref, *banks
 ):
     step = pl.program_id(0)
     last = pl.num_programs(0) - 1
     unknowns = tiles_ref.shape[0]
-    rounds = 8
+    rounds = 2
     pairs = BLOCK // 2 // rounds
 
     @pl.when(step == 0)
@@ -150,7 +151,7 @@
                 if applying:
                     apply_four(
                         True, (step - 1) * BLOCK, g * pairs + u,
-                        pick_s, put_s, flag_s, held_ref, near_ref, banks
+                        index_s, held_ref, near_ref, banks
                     )
             return carry
 
@@ -174,7 +175,7 @@
         pack_slots(banks, out_ref, unknowns, capacity)
 
 
-def first_pass(pick, put, flag, tiles, table, rows, capacity):
+def first_pass(index, tiles, table, rows, capacity):
     count, unknowns = tiles.shape[0], tiles.shape[1]
     blocks = count // BLOCK
     out = (rows * unknowns // LANES, NRHS, LANES)
@@ -186,7 +187,7 @@
             jax.ShapeDtypeStruct(out, jnp.float32),
         ],
         grid_spec=pltpu.PrefetchScalarGridSpec(
-            num_scalar_prefetch=3,
+            num_scalar_prefetch=1,
             grid=(blocks + 1,),
             in_specs=[
                 pl.BlockSpec(
@@ -212,10 +213,10 @@
             transcendentals=0,
         ),
         name="pair_and_mirror",
-    )(pick, put, flag, jnp.transpose(tiles, (1, 2, 0)), table)
-
-
-def tile_pass(mirrored, pick, put, flag, pairs, table, rows, capacity):
+    )(index, jnp.transpose(tiles, (1, 2, 0)), table)
+
+
+def tile_pass(mirrored, index, pairs, table, rows, capacity):
     count, unknowns = 2 * pairs.shape[0], pairs.shape[1]
     near = (2, table.shape[0], NRHS, 2 * unknowns) if mirrored else (1, table.shape[0], NRHS, LANES)
     widths = (LANES,) * BANKS if mirrored else (LANES, LANES, 2 * unknowns, 2 * unknowns)
@@ -227,7 +228,7 @@
         functools.partial(pass_kernel, mirrored, capacity),
         out_shape=jax.ShapeDtypeStruct(out, jnp.float32),
         grid_spec=pltpu.PrefetchScalarGridSpec(
-            num_scalar_prefetch=3,
+            num_scalar_prefetch=1,
             grid=(count // BLOCK,),
             in_specs=[
                 pl.BlockSpec((BLOCK // 2, unknowns, 2 * LANES), lambda s, *_: (s, 0, 0)),
@@ -244,7 +245,7 @@
             transcendentals=0,
         ),
         name="mirror_pass" if mirrored else "direct_pass",
-    )(pick, put, flag, pairs, table)
+    )(index, pairs, table)
 
 
 def gather_kernel(row_s, from_ref, out_ref, wide_ref):
@@ -296,7 +297,7 @@
             banks[c % BANKS][row_s[p * capacity + c]] += got
         return carry
 
-    lax.fori_loop(0, got_ref.shape[0] // kept, peer, 0)
+    lax.fori_loop(0, got_ref.shape[0] // kept, peer, 0, unroll=4)
     total = banks[0][...]
     for bank in banks[1:]:
         total += bank[...]
@@ -330,18 +331,21 @@
     slots = peers * capacity
     wanted = want_list[0]
     start = forces.reshape(fibres, NRHS, unknowns)
-    asked = lax.all_to_all(wanted, "row", 0, 0, tiled=True).reshape(-1)
+    index = jnp.concatenate([tile_local, tile_slot, tile_flag])
+    asked = lax.all_to_all(wanted, "row", 0, 0, tiled=True)
+    asked, index = lax.optimization_barrier((asked, index))
+    asked = asked.reshape(-1)
     first_sent, start = lax.optimization_barrier((gather(asked, start), start))
-    pairs, mirrored = first_pass(tile_local, tile_slot, tile_flag, tiles, start, slots, capacity)
+    pairs, mirrored = first_pass(index, tiles, start, slots, capacity)
 
     def finish(mirrored, sent, again):
         got = lax.all_to_all(mirrored, "row", 0, 0, tiled=True)
         far = lax.all_to_all(sent, "row", 0, 0, tiled=True)
-        own = tile_pass(False, tile_slot, tile_local, tile_flag, pairs, far, fibres, capacity)
+        own = tile_pass(False, index, pairs, far, fibres, capacity)
         return combine(asked, own, got, capacity, again)
 
     one, sent = finish(mirrored, first_sent, True)
-    mirrored = tile_pass(True, tile_local, tile_slot, tile_flag, pairs, one, slots, capacity)
+    mirrored = tile_pass(True, index, pairs, one, slots, capacity)
     (two,) = finish(mirrored, sent, False)
     return (one.reshape(fibres, width), two.reshape(fibres, width))
 

time: 133 us -> 121 us (0.910)
  Pallas kernels: 85.4 us -> 75.2 us
  local copies, waits for them, and re-layouts: 7.33 us -> 2.69 us
  waiting for transfers between devices: 9.49 us -> 11.8 us
    pallas_call x1, Pallas kernels: 31.3 us -> 25.6 us  [first_pass(): pl.pallas_call(functools.partial(first_kernel, capacity), out_shape=[jax....]
    unnamed x18 -> x0, local copies, waits for them, and re-layouts: 4.12 us -> none
    pallas_call x3, Pallas kernels: 47.3 us -> 44.2 us  [tile_pass(): pl.pallas_call(functools.partial(pass_kernel, mirrored, capacity), out_sh...]
    all_to_all x2, waiting for transfers between devices: 5.92 us -> 8.92 us  [finish(): got = lax.all_to_all(mirrored, 'row', 0, 0, tiled=True)]
    pallas_call x2, Pallas kernels: 5.09 us -> 3.66 us  [combine(): pl.pallas_call(functools.partial(combine_kernel, capacity), out_shape=out...]
  transfers between devices with their start and end apart: 5 -> 5, of which waited for: 3 -> 3; matrix products, arithmetic and copies ran while one was open for 1% -> 2% of each run, Pallas kernels for 59% -> 58%
where the time goes in v7:
time: 121 us; the launch traced here: 120 us
  Pallas kernels  75.2 us (62%)
  starting transfers between devices  28.5 us (24%)
  waiting for transfers between devices  11.8 us (10%)
  local copies, waits for them, and re-layouts  2.69 us (2%)
    pallas_call x3, Pallas kernels, tile_pass(): pl.pallas_call(functools.partial(pass_kernel, mirrored, capacity), out_sh...  44.2 us
    pallas_call x1, Pallas kernels, first_pass(): pl.pallas_call(functools.partial(first_kernel, capacity), out_shape=[jax....  25.6 us
    all_to_all x2, starting transfers between devices, finish(): got = lax.all_to_all(mirrored, 'row', 0, 0, tiled=True)  12.1 us
    all_to_all x2, starting transfers between devices, finish(): far = lax.all_to_all(sent, 'row', 0, 0, tiled=True)  9.82 us
    all_to_all x2, waiting for transfers between devices, finish(): got = lax.all_to_all(mirrored, 'row', 0, 0, tiled=True)  8.92 us
    all_to_all x1, starting transfers between devices, per_device(): asked = lax.all_to_all(wanted, 'row', 0, 0, tiled=True)  6.62 us
    pallas_call x2, Pallas kernels, combine(): pl.pallas_call(functools.partial(combine_kernel, capacity), out_shape=out...  3.66 us
    all_to_all x1, waiting for transfers between devices, per_device(): asked = lax.all_to_all(wanted, 'row', 0, 0, tiled=True)  2.84 us
  transfers between devices with their start and end apart: 5, of which 3 were waited for; matrix products, arithmetic and copies ran while one was open for 2% of the time, Pallas kernels for 58%

profile of v7, /device:TPU:9, one launch (start us, length us, event | category | flops | bytes accessed | tf_op | source)
XLA Modules:
  0.0 119.6 jit_solution(5124931219273668085)
XLA Ops:
  0.6 6.6 %all-to-all-start = ((s32[16,1,16]{2,1,0:T(1,128)}), s32[16,1,16]{2,1,0:T(1,128)S(1)}, u32[]{:S(2)}, u32[]{:S(2)}) async-start(s32[16,1,16]{2,1,0:T(1,128)} %bitcast.5), calls=%async_computation | async-start | bytes 16384 | tf_op jit(solution)/shard_map/all_to_all | solution.py:335
  7.3 0.7 pad_add_fusion.index_s
  8.0 1.0 reshape.20.from_ref.table_ref
  9.0 2.8 %all-to-all-done = s32[16,1,16]{2,1,0:T(1,128)S(1)} async-done(((s32[16,1,16]{2,1,0:T(1,128)}), s32[16,1,16]{2,1,0:T(1,128)S(1)}, u32[]{:S(2)}, u32[]{:S(2)}) %all-to-all-start) | async-done | bytes 1056 | tf_op jit(solution)/shard_map/all_to_all | solution.py:335
  11.9 0.1 reshape.19.row_s
  11.9 1.7 %gather_rows.1 = bf16[256,8,96]{2,1,0:T(8,128)(2,1)} custom-call(s32[256]{0:T(256)S(1)} %reshape.19.row_s, bf16[64,8,96]{2,1,0:T(8,128)(2,1)S(1)} %reshape.20.from_ref.table_ref), custom_call_target="tpu_custom_call" | custom-call | tf_op jit(solution)/shard_map/gather_rows/pallas_call | solution.py:268
  13.7 5.2 %all-to-all-start.1 = ((bf16[256,8,96]{2,1,0:T(8,128)(2,1)}), bf16[256,8,96]{2,1,0:T(8,128)(2,1)S(1)}, u32[]{:S(2)}, u32[]{:S(2)}) async-start(bf16[256,8,96]{2,1,0:T(8,128)(2,1)} %gather_rows.1), calls=%async_computation.1 | async-start | bytes 1048576 | tf_op jit(solution)/shard_map/all_to_all | solution.py:343
  18.9 25.6 %pair_and_mirror.1 = (bf16[512,96,256]{2,1,0:T(8,128)(2,1)}, f32[192,8,128]{2,1,0:T(8,128)}) custom-call(s32[3072]{0:T(1024)S(1)} %pad_add_fusion.index_s, bf16[96,96,1024]{2,1,0:T(8,128)(2,1)} %bitcast.3, bf16[64,8,96]{2,1,0:T(8,128)(2,1)S(1)} %reshape.20.from_ref.table_ref), custom_call_target="tpu_custom_call" | custom-call | flops 150994944 | bytes 46137344 | tf_op jit(solution)/shard_map/pair_and_mirror/pallas_call | solution.py:183
  44.5 0.0 all-to-all-done.1.table_ref
  44.5 6.1 %all-to-all-start.2 = ((f32[192,8,128]{2,1,0:T(8,128)}), f32[192,8,128]{2,1,0:T(8,128)S(1)}, u32[]{:S(2)}, u32[]{:S(2)}) async-start(f32[192,8,128]{2,1,0:T(8,128)} %get-tuple-element.15), calls=%async_computation.2 | async-start | bytes 1572864 | tf_op jit(solution)/shard_map/all_to_all | solution.py:342
  50.6 14.7 %direct_pass.2.own_ref = f32[64,8,96]{2,1,0:T(8,128)S(1)} custom-call(s32[3072]{0:T(1024)S(1)} %pad_add_fusion.index_s, bf16[512,96,256]{2,1,0:T(8,128)(2,1)} %get-tuple-element.13.pairs_ref, bf16[256,8,96]{2,1,0:T(8,128)(2,1)S(1)} %all-to-all-done.1.table_ref), custom_call_target="tpu_custom_call" | custom-call | flops 150994944 | bytes 25165824 | tf_op jit(solution)/shard_map/direct_pass/pallas_call | solution.py:227
  65.3 4.9 %all-to-all-done.2.got_ref = f32[192,8,128]{2,1,0:T(8,128)S(1)} async-done(((f32[192,8,128]{2,1,0:T(8,128)}), f32[192,8,128]{2,1,0:T(8,128)S(1)}, u32[]{:S(2)}, u32[]{:S(2)}) %all-to-all-start.2) | async-done | bytes 786464 | tf_op jit(solution)/shard_map/all_to_all | solution.py:342
  70.2 2.4 %combine_rows.2 = (bf16[64,8,96]{2,1,0:T(8,128)(2,1)S(1)}, bf16[256,8,96]{2,1,0:T(8,128)(2,1)}) custom-call(s32[256]{0:T(256)S(1)} %reshape.19.row_s, f32[64,8,96]{2,1,0:T(8,128)S(1)} %direct_pass.2.own_ref, f32[192,8,128]{2,1,0:T(8,128)S(1)} %all-to-all-done.2.got_ref), custom_call_target="tpu_custom_call" | custom-call | tf_op jit(solution)/shard_map/combine_rows/pallas_call | solution.py:315
  72.6 4.6 %all-to-all-start.3 = ((bf16[256,8,96]{2,1,0:T(8,128)(2,1)}), bf16[256,8,96]{2,1,0:T(8,128)(2,1)S(1)}, u32[]{:S(2)}, u32[]{:S(2)}) async-start(bf16[256,8,96]{2,1,0:T(8,128)(2,1)} %get-tuple-element.17), calls=%async_computation.3 | async-start | bytes 1048576 | tf_op jit(solution)/shard_map/all_to_all | solution.py:343
  77.2 14.8 %mirror_pass.1 = f32[192,8,128]{2,1,0:T(8,128)} custom-call(s32[3072]{0:T(1024)S(1)} %pad_add_fusion.index_s, bf16[512,96,256]{2,1,0:T(8,128)(2,1)} %get-tuple-element.13.pairs_ref, bf16[64,8,96]{2,1,0:T(8,128)(2,1)S(1)} %get-tuple-element.16.table_ref), custom_call_target="tpu_custom_call" | custom-call | flops 150994944 | bytes 25165824 | tf_op jit(solution)/shard_map/mirror_pass/pallas_call | solution.py:227
  92.0 0.0 all-to-all-done.3.table_ref
  92.0 6.0 %all-to-all-start.4 = ((f32[192,8,128]{2,1,0:T(8,128)}), f32[192,8,128]{2,1,0:T(8,128)S(1)}, u32[]{:S(2)}, u32[]{:S(2)}) async-start(f32[192,8,128]{2,1,0:T(8,128)} %mirror_pass.1), calls=%async_computation.4 | async-start | bytes 1572864 | tf_op jit(solution)/shard_map/all_to_all | solution.py:342
  98.0 0.8 reshape.21
  98.8 14.7 %direct_pass.3.own_ref = f32[64,8,96]{2,1,0:T(8,128)S(1)} custom-call(s32[3072]{0:T(1024)S(1)} %pad_add_fusion.index_s, bf16[512,96,256]{2,1,0:T(8,128)(2,1)} %get-tuple-element.13.pairs_ref, bf16[256,8,96]{2,1,0:T(8,128)(2,1)S(1)} %all-to-all-done.3.table_ref), custom_call_target="tpu_custom_call" | custom-call | flops 150994944 | bytes 25165824 | tf_op jit(solution)/shard_map/direct_pass/pallas_call | solution.py:227
  113.5 4.1 %all-to-all-done.4.got_ref = f32[192,8,128]{2,1,0:T(8,128)S(1)} async-done(((f32[192,8,128]{2,1,0:T(8,128)}), f32[192,8,128]{2,1,0:T(8,128)S(1)}, u32[]{:S(2)}, u32[]{:S(2)}) %all-to-all-start.4) | async-done | bytes 786464 | tf_op jit(solution)/shard_map/all_to_all | solution.py:342
  117.6 1.2 %combine_rows.3 = bf16[64,8,96]{2,1,0:T(8,128)(2,1)S(1)} custom-call(s32[256]{0:T(256)S(1)} %reshape.19.row_s, f32[64,8,96]{2,1,0:T(8,128)S(1)} %direct_pass.3.own_ref, f32[192,8,128]{2,1,0:T(8,128)S(1)} %all-to-all-done.4.got_ref), custom_call_target="tpu_custom_call" | custom-call | tf_op jit(solution)/shard_map/combine_rows/pallas_call | solution.py:315
  118.8 0.8 reshape.22
Async XLA Ops:
  0.6 11.2 %all-to-all-start = ((s32[16,1,16]{2,1,0:T(1,128)}), s32[16,1,16]{2,1,0:T(1,128)S(1)}, u32[]{:S(2)}, u32[]{:S(2)}) async-start(s32[16,1,16]{2,1,0:T(1,128)} %bitcast.5), calls=%async_computation | async-start | bytes 16384 | tf_op jit(solution)/shard_map/all_to_all | solution.py:335
  13.7 30.8 %all-to-all-start.1 = ((bf16[256,8,96]{2,1,0:T(8,128)(2,1)}), bf16[256,8,96]{2,1,0:T(8,128)(2,1)S(1)}, u32[]{:S(2)}, u32[]{:S(2)}) async-start(bf16[256,8,96]{2,1,0:T(8,128)(2,1)} %gather_rows.1), calls=%async_computation.1 | async-start | bytes 1048576 | tf_op jit(solution)/shard_map/all_to_all | solution.py:343
  44.5 25.6 %all-to-all-start.2 = ((f32[192,8,128]{2,1,0:T(8,128)}), f32[192,8,128]{2,1,0:T(8,128)S(1)}, u32[]{:S(2)}, u32[]{:S(2)}) async-start(f32[192,8,128]{2,1,0:T(8,128)} %get-tuple-element.15), calls=%async_computation.2 | async-start | bytes 1572864 | tf_op jit(solution)/shard_map/all_to_all | solution.py:342
  72.6 19.4 %all-to-all-start.3 = ((bf16[256,8,96]{2,1,0:T(8,128)(2,1)}), bf16[256,8,96]{2,1,0:T(8,128)(2,1)S(1)}, u32[]{:S(2)}, u32[]{:S(2)}) async-start(bf16[256,8,96]{2,1,0:T(8,128)(2,1)} %get-tuple-element.17), calls=%async_computation.3 | async-start | bytes 1048576 | tf_op jit(solution)/shard_map/all_to_all | solution.py:343
  92.0 25.6 %all-to-all-start.4 = ((f32[192,8,128]{2,1,0:T(8,128)}), f32[192,8,128]{2,1,0:T(8,128)S(1)}, u32[]{:S(2)}, u32[]{:S(2)}) async-start(f32[192,8,128]{2,1,0:T(8,128)} %mirror_pass.1), calls=%async_computation.4 | async-start | bytes 1572864 | tf_op jit(solution)/shard_map/all_to_all | solution.py:342

commit v8 on v7

--- a/solution.py
+++ b/solution.py
@@ -9,7 +9,7 @@
 
 NRHS = 8
 BANKS = 4
-UNROLL = 128
+JOINED = 2
 LANES = 128
 ROWS = 16
 BLOCK = 128
@@ -107,15 +107,11 @@
     def _():
         prepare(mirrored, table_ref, near_ref, banks)
 
-    def group(g, carry):
-        start = pl.multiple_of(g * (UNROLL // 2), UNROLL // 2)
-        for u in range(0, UNROLL // 2, 2):
-            apply_four(
-                mirrored, step * BLOCK, start + u, index_s, pairs_ref, near_ref, banks
-            )
-        return carry
-
-    lax.fori_loop(0, BLOCK // UNROLL, group, 0)
+    half = BLOCK // 2
+    for b in range(JOINED):
+        view = pairs_ref.at[pl.ds(b * half, half)]
+        for p in range(0, half, 2):
+            apply_four(mirrored, (step * JOINED + b) * BLOCK, p, index_s, view, near_ref, banks)
 
     @pl.when(step == pl.num_programs(0) - 1)
     def _():
@@ -133,7 +129,7 @@
     step = pl.program_id(0)
     last = pl.num_programs(0) - 1
     unknowns = tiles_ref.shape[0]
-    rounds = 2
+    rounds = 1
     pairs = BLOCK // 2 // rounds
 
     @pl.when(step == 0)
@@ -229,9 +225,9 @@
         out_shape=jax.ShapeDtypeStruct(out, jnp.float32),
         grid_spec=pltpu.PrefetchScalarGridSpec(
             num_scalar_prefetch=1,
-            grid=(count // BLOCK,),
+            grid=(count // (JOINED * BLOCK),),
             in_specs=[
-                pl.BlockSpec((BLOCK // 2, unknowns, 2 * LANES), lambda s, *_: (s, 0, 0)),
+                pl.BlockSpec((JOINED * BLOCK // 2, unknowns, 2 * LANES), lambda s, *_: (s, 0, 0)),
                 pl.BlockSpec(table.shape, lambda s, *_: (0, 0, 0)),
             ],
             out_specs=pl.BlockSpec(out, lambda s, *_: (0, 0, 0)),

time: 121 us -> 119 us (0.983)
  Pallas kernels: 75.2 us -> 70.1 us
  waiting for transfers between devices: 11.8 us -> 15.8 us
    pallas_call x3, Pallas kernels: 44.2 us -> 39.5 us  [tile_pass(): pl.pallas_call(functools.partial(pass_kernel, mirrored, capacity), out_sh...]
    all_to_all x2, waiting for transfers between devices: 8.92 us -> 11.9 us  [finish(): got = lax.all_to_all(mirrored, 'row', 0, 0, tiled=True)]
  transfers between devices with their start and end apart: 5 -> 5, of which waited for: 3 -> 4; matrix products, arithmetic and copies ran while one was open for 2% -> 2% of each run, Pallas kernels for 58% -> 55%
where the time goes in v8:
time: 119 us; the launch traced here: 118 us
  Pallas kernels  70.1 us (59%)
  starting transfers between devices  27.5 us (23%)
  waiting for transfers between devices  15.8 us (13%)
  local copies, waits for them, and re-layouts  2.69 us (2%)
    pallas_call x3, Pallas kernels, tile_pass(): pl.pallas_call(functools.partial(pass_kernel, mirrored, capacity), out_sh...  39.5 us
    pallas_call x1, Pallas kernels, first_pass(): pl.pallas_call(functools.partial(first_kernel, capacity), out_shape=[jax....  25.3 us
    all_to_all x2, waiting for transfers between devices, finish(): got = lax.all_to_all(mirrored, 'row', 0, 0, tiled=True)  11.9 us
    all_to_all x2, starting transfers between devices, finish(): got = lax.all_to_all(mirrored, 'row', 0, 0, tiled=True)  11 us
    all_to_all x2, starting transfers between devices, finish(): far = lax.all_to_all(sent, 'row', 0, 0, tiled=True)  9.83 us
    all_to_all x1, starting transfers between devices, per_device(): asked = lax.all_to_all(wanted, 'row', 0, 0, tiled=True)  6.62 us
    pallas_call x2, Pallas kernels, combine(): pl.pallas_call(functools.partial(combine_kernel, capacity), out_shape=out...  3.65 us
    all_to_all x1, waiting for transfers between devices, per_device(): asked = lax.all_to_all(wanted, 'row', 0, 0, tiled=True)  2.84 us
  transfers between devices with their start and end apart: 5, of which 4 were waited for; matrix products, arithmetic and copies ran while one was open for 2% of the time, Pallas kernels for 55%

profile of v8, /device:TPU:9, one launch (start us, length us, event | category | flops | bytes accessed | tf_op | source)
XLA Modules:
  0.0 117.5 jit_solution(6442782738021623865)
XLA Ops:
  0.6 6.6 %all-to-all-start = ((s32[16,1,16]{2,1,0:T(1,128)}), s32[16,1,16]{2,1,0:T(1,128)S(1)}, u32[]{:S(2)}, u32[]{:S(2)}) async-start(s32[16,1,16]{2,1,0:T(1,128)} %bitcast.5), calls=%async_computation | async-start | bytes 16384 | tf_op jit(solution)/shard_map/all_to_all | solution.py:331
  7.3 0.7 pad_add_fusion.index_s
  8.0 1.0 reshape.20.from_ref.table_ref
  9.0 2.8 %all-to-all-done = s32[16,1,16]{2,1,0:T(1,128)S(1)} async-done(((s32[16,1,16]{2,1,0:T(1,128)}), s32[16,1,16]{2,1,0:T(1,128)S(1)}, u32[]{:S(2)}, u32[]{:S(2)}) %all-to-all-start) | async-done | bytes 1056 | tf_op jit(solution)/shard_map/all_to_all | solution.py:331
  11.9 0.1 reshape.19.row_s
  11.9 1.7 %gather_rows.1 = bf16[256,8,96]{2,1,0:T(8,128)(2,1)} custom-call(s32[256]{0:T(256)S(1)} %reshape.19.row_s, bf16[64,8,96]{2,1,0:T(8,128)(2,1)S(1)} %reshape.20.from_ref.table_ref), custom_call_target="tpu_custom_call" | custom-call | tf_op jit(solution)/shard_map/gather_rows/pallas_call | solution.py:264
  13.7 5.2 %all-to-all-start.1 = ((bf16[256,8,96]{2,1,0:T(8,128)(2,1)}), bf16[256,8,96]{2,1,0:T(8,128)(2,1)S(1)}, u32[]{:S(2)}, u32[]{:S(2)}) async-start(bf16[256,8,96]{2,1,0:T(8,128)(2,1)} %gather_rows.1), calls=%async_computation.1 | async-start | bytes 1048576 | tf_op jit(solution)/shard_map/all_to_all | solution.py:339
  18.9 25.3 %pair_and_mirror.1 = (bf16[512,96,256]{2,1,0:T(8,128)(2,1)}, f32[192,8,128]{2,1,0:T(8,128)}) custom-call(s32[3072]{0:T(1024)S(1)} %pad_add_fusion.index_s, bf16[96,96,1024]{2,1,0:T(8,128)(2,1)} %bitcast.3, bf16[64,8,96]{2,1,0:T(8,128)(2,1)S(1)} %reshape.20.from_ref.table_ref), custom_call_target="tpu_custom_call" | custom-call | flops 150994944 | bytes 46137344 | tf_op jit(solution)/shard_map/pair_and_mirror/pallas_call | solution.py:179
  44.2 0.0 all-to-all-done.1.table_ref
  44.2 6.1 %all-to-all-start.2 = ((f32[192,8,128]{2,1,0:T(8,128)}), f32[192,8,128]{2,1,0:T(8,128)S(1)}, u32[]{:S(2)}, u32[]{:S(2)}) async-start(f32[192,8,128]{2,1,0:T(8,128)} %get-tuple-element.15), calls=%async_computation.2 | async-start | bytes 1572864 | tf_op jit(solution)/shard_map/all_to_all | solution.py:338
  50.2 13.2 %direct_pass.2.own_ref = f32[64,8,96]{2,1,0:T(8,128)S(1)} custom-call(s32[3072]{0:T(1024)S(1)} %pad_add_fusion.index_s, bf16[512,96,256]{2,1,0:T(8,128)(2,1)} %get-tuple-element.13.pairs_ref, bf16[256,8,96]{2,1,0:T(8,128)(2,1)S(1)} %all-to-all-done.1.table_ref), custom_call_target="tpu_custom_call" | custom-call | flops 150994944 | bytes 25165824 | tf_op jit(solution)/shard_map/direct_pass/pallas_call | solution.py:223
  63.5 6.3 %all-to-all-done.2.got_ref = f32[192,8,128]{2,1,0:T(8,128)S(1)} async-done(((f32[192,8,128]{2,1,0:T(8,128)}), f32[192,8,128]{2,1,0:T(8,128)S(1)}, u32[]{:S(2)}, u32[]{:S(2)}) %all-to-all-start.2) | async-done | bytes 786464 | tf_op jit(solution)/shard_map/all_to_all | solution.py:338
  69.8 2.4 %combine_rows.2 = (bf16[64,8,96]{2,1,0:T(8,128)(2,1)S(1)}, bf16[256,8,96]{2,1,0:T(8,128)(2,1)}) custom-call(s32[256]{0:T(256)S(1)} %reshape.19.row_s, f32[64,8,96]{2,1,0:T(8,128)S(1)} %direct_pass.2.own_ref, f32[192,8,128]{2,1,0:T(8,128)S(1)} %all-to-all-done.2.got_ref), custom_call_target="tpu_custom_call" | custom-call | tf_op jit(solution)/shard_map/combine_rows/pallas_call | solution.py:311
  72.2 4.6 %all-to-all-start.3 = ((bf16[256,8,96]{2,1,0:T(8,128)(2,1)}), bf16[256,8,96]{2,1,0:T(8,128)(2,1)S(1)}, u32[]{:S(2)}, u32[]{:S(2)}) async-start(bf16[256,8,96]{2,1,0:T(8,128)(2,1)} %get-tuple-element.17), calls=%async_computation.3 | async-start | bytes 1048576 | tf_op jit(solution)/shard_map/all_to_all | solution.py:339
  76.8 13.1 %mirror_pass.1 = f32[192,8,128]{2,1,0:T(8,128)} custom-call(s32[3072]{0:T(1024)S(1)} %pad_add_fusion.index_s, bf16[512,96,256]{2,1,0:T(8,128)(2,1)} %get-tuple-element.13.pairs_ref, bf16[64,8,96]{2,1,0:T(8,128)(2,1)S(1)} %get-tuple-element.16.table_ref), custom_call_target="tpu_custom_call" | custom-call | flops 150994944 | bytes 25165824 | tf_op jit(solution)/shard_map/mirror_pass/pallas_call | solution.py:223
  89.9 1.1 all-to-all-done.3.table_ref
  91.0 5.0 %all-to-all-start.4 = ((f32[192,8,128]{2,1,0:T(8,128)}), f32[192,8,128]{2,1,0:T(8,128)S(1)}, u32[]{:S(2)}, u32[]{:S(2)}) async-start(f32[192,8,128]{2,1,0:T(8,128)} %mirror_pass.1), calls=%async_computation.4 | async-start | bytes 1572864 | tf_op jit(solution)/shard_map/all_to_all | solution.py:338
  95.9 0.8 reshape.21
  96.7 13.2 %direct_pass.3.own_ref = f32[64,8,96]{2,1,0:T(8,128)S(1)} custom-call(s32[3072]{0:T(1024)S(1)} %pad_add_fusion.index_s, bf16[512,96,256]{2,1,0:T(8,128)(2,1)} %get-tuple-element.13.pairs_ref, bf16[256,8,96]{2,1,0:T(8,128)(2,1)S(1)} %all-to-all-done.3.table_ref), custom_call_target="tpu_custom_call" | custom-call | flops 150994944 | bytes 25165824 | tf_op jit(solution)/shard_map/direct_pass/pallas_call | solution.py:223
  109.9 5.6 %all-to-all-done.4.got_ref = f32[192,8,128]{2,1,0:T(8,128)S(1)} async-done(((f32[192,8,128]{2,1,0:T(8,128)}), f32[192,8,128]{2,1,0:T(8,128)S(1)}, u32[]{:S(2)}, u32[]{:S(2)}) %all-to-all-start.4) | async-done | bytes 786464 | tf_op jit(solution)/shard_map/all_to_all | solution.py:338
  115.5 1.2 %combine_rows.3 = bf16[64,8,96]{2,1,0:T(8,128)(2,1)S(1)} custom-call(s32[256]{0:T(256)S(1)} %reshape.19.row_s, f32[64,8,96]{2,1,0:T(8,128)S(1)} %direct_pass.3.own_ref, f32[192,8,128]{2,1,0:T(8,128)S(1)} %all-to-all-done.4.got_ref), custom_call_target="tpu_custom_call" | custom-call | tf_op jit(solution)/shard_map/combine_rows/pallas_call | solution.py:311
  116.7 0.8 reshape.22
Async XLA Ops:
  0.6 11.2 %all-to-all-start = ((s32[16,1,16]{2,1,0:T(1,128)}), s32[16,1,16]{2,1,0:T(1,128)S(1)}, u32[]{:S(2)}, u32[]{:S(2)}) async-start(s32[16,1,16]{2,1,0:T(1,128)} %bitcast.5), calls=%async_computation | async-start | bytes 16384 | tf_op jit(solution)/shard_map/all_to_all | solution.py:331
  13.7 30.5 %all-to-all-start.1 = ((bf16[256,8,96]{2,1,0:T(8,128)(2,1)}), bf16[256,8,96]{2,1,0:T(8,128)(2,1)S(1)}, u32[]{:S(2)}, u32[]{:S(2)}) async-start(bf16[256,8,96]{2,1,0:T(8,128)(2,1)} %gather_rows.1), calls=%async_computation.1 | async-start | bytes 1048576 | tf_op jit(solution)/shard_map/all_to_all | solution.py:339
  44.2 25.6 %all-to-all-start.2 = ((f32[192,8,128]{2,1,0:T(8,128)}), f32[192,8,128]{2,1,0:T(8,128)S(1)}, u32[]{:S(2)}, u32[]{:S(2)}) async-start(f32[192,8,128]{2,1,0:T(8,128)} %get-tuple-element.15), calls=%async_computation.2 | async-start | bytes 1572864 | tf_op jit(solution)/shard_map/all_to_all | solution.py:338
  72.2 18.8 %all-to-all-start.3 = ((bf16[256,8,96]{2,1,0:T(8,128)(2,1)}), bf16[256,8,96]{2,1,0:T(8,128)(2,1)S(1)}, u32[]{:S(2)}, u32[]{:S(2)}) async-start(bf16[256,8,96]{2,1,0:T(8,128)(2,1)} %get-tuple-element.17), calls=%async_computation.3 | async-start | bytes 1048576 | tf_op jit(solution)/shard_map/all_to_all | solution.py:339
  91.0 24.5 %all-to-all-start.4 = ((f32[192,8,128]{2,1,0:T(8,128)}), f32[192,8,128]{2,1,0:T(8,128)S(1)}, u32[]{:S(2)}, u32[]{:S(2)}) async-start(f32[192,8,128]{2,1,0:T(8,128)} %mirror_pass.1), calls=%async_computation.4 | async-start | bytes 1572864 | tf_op jit(solution)/shard_map/all_to_all | solution.py:338
